TPU v7x, 512 devices: a whole 4x4x16 slice. The times are simulated.
512 devices in a mesh: slab: 128 (over y, z, core), sub: 4 (over x).
Axes of the slice: x: 4, y: 4, z: 16, core: 2. Of those that a mesh axis runs over, the one named last changes fastest.
Arguments:
- coefficients: bfloat16 [7, 6, 6, 1024, 12, 128], P(None, None, None, 'slab', 'sub'), may hold values from -1 to 1
- earlier: float32 [30, 6, 1024, 12, 128], P(None, None, 'slab', 'sub'), may hold values from -6 to 6
- start: float32 [6, 1024, 12, 128], P(None, 'slab', 'sub'), may hold values from -8 to 8
- shifts: float32 [5], replicated, may hold values from -0.3 to 0.3
Outputs:
- new_basis: float32 [6, 6, 1024, 12, 128], P(None, None, 'slab', 'sub')
- projection: float32 [30, 6], replicated
- triangle: float32 [6, 6], replicated
All inputs are finite; a program needn't handle non-finite values.
Results may differ from a plain program's by a relative error of at most 0.0015.
Values may be sent and summed in bfloat16 or wider, within the bound.
No kernel may reach another device: no remote copies, remote signals or barrier semaphores. Data moves between devices by JAX's collectives and lax.ppermute only.
A program may use at most 64 MiB of HBM per device.

v0:
```python
import jax
import jax.numpy as jnp
from jax import lax
from jax.sharding import Mesh
from jax.sharding import PartitionSpec as P

SLAB = ("slab_0", "slab_1", "slab_2")


def padded_2(x, sides, width):
    edges = {}
    for axis, dim in sides:
        count, length = (lax.axis_size(axis), x.shape[dim])
        up = [(i, (i + 1) % count) for i in range(count - 1)]
        last = lax.slice_in_dim(x, length - width, length, axis=dim)
        first = lax.slice_in_dim(x, 0, width, axis=dim)
        edges[dim] = (
            lax.ppermute(last, axis, up),
            lax.ppermute(first, axis, [(b, a) for a, b in up]),
        )
    done = []
    for _, dim in sides:
        low, high = edges[dim]
        around = [(width, width) if d in done else (0, 0) for d in range(x.ndim)]
        x = jnp.concatenate([jnp.pad(low, around), x, jnp.pad(high, around)], axis=dim)
        done.append(dim)
    return x


def copy_for_each(x, axis):
    copies = jnp.broadcast_to(x, (lax.axis_size(axis), *x.shape))
    return lax.all_to_all(copies, axis, split_axis=0, concat_axis=0, tiled=True)


def over_copies(x, axis):
    everything = copy_for_each(x, axis)
    return jnp.sum(everything, axis=0)


def one_axis_at_a_time(x, axes):
    far, near = axes
    nearer = over_copies(x, near)
    return over_copies(nearer, far)


def packed_total(arrays, axis):
    ravelled, at, done = (jnp.concatenate([a.reshape(-1) for a in arrays]), 0, [])
    so_far = one_axis_at_a_time(ravelled, axis)
    for a in arrays:
        done.append(so_far[at : at + a.size].reshape(a.shape))
        at += a.size
    return tuple(done)


def nearby_fields(padded):
    center = padded[:, 1:-1, 1:-1]
    zeros_edge = jnp.zeros_like(center[..., :1])
    lower_y = jnp.concatenate([zeros_edge, center[..., :-1]], axis=3)
    upper_y = jnp.concatenate([center[..., 1:], zeros_edge], axis=3)
    return [
        center,
        padded[:, :-2, 1:-1],
        padded[:, 2:, 1:-1],
        padded[:, 1:-1, :-2],
        padded[:, 1:-1, 2:],
        lower_y,
        upper_y,
    ]


def apply_padded(coefficients, padded, theta):
    fields = nearby_fields(padded)
    result = (1.0 - theta) * fields[0]
    for coupling in range(len(fields)):
        result = result + jnp.sum(coefficients[coupling] * fields[coupling][None], axis=1)
    return result


def body(coefficients, earlier, start, shifts):
    depth = shifts.shape[0]
    vectors = [start]
    current = start
    for step in range(depth):
        padded = padded_2(current, ((SLAB, 1), ("sub", 2)), 1)
        current = apply_padded(coefficients, padded, shifts[step])
        vectors.append(current)
    basis = jnp.stack(vectors)
    block_count = basis.shape[0]
    flat = basis.reshape(block_count, -1)
    earlier_flat = earlier.reshape(earlier.shape[0], -1)
    count = flat.shape[1] * lax.axis_size(SLAB) * lax.axis_size("sub")
    local_cross = jnp.dot(earlier_flat, flat.T, precision=lax.Precision.HIGHEST)
    local_self = jnp.dot(flat, flat.T, precision=lax.Precision.HIGHEST)
    local_earlier = jnp.dot(earlier_flat, earlier_flat.T, precision=lax.Precision.HIGHEST)
    cross_sum, self_sum, earlier_sum = packed_total(
        (local_cross, local_self, local_earlier), (("slab_0", "slab_1"), ("slab_2", "sub"))
    )
    projection = cross_sum / count
    rest = flat - jnp.dot(projection.T, earlier_flat, precision=lax.Precision.HIGHEST)
    weighted = jnp.dot(earlier_sum / count, projection, precision=lax.Precision.HIGHEST)
    gram = self_sum / count - 2.0 * jnp.dot(
        projection.T, projection, precision=lax.Precision.HIGHEST
    )
    gram = gram + jnp.dot(projection.T, weighted, precision=lax.Precision.HIGHEST)
    lower = jnp.linalg.cholesky(gram)
    new_flat = lax.linalg.triangular_solve(lower, rest, left_side=True, lower=True)
    return (new_flat.reshape(basis.shape), projection, lower.T)


def solution(mesh):
    torus = Mesh(
        mesh.devices.reshape(4, 16, 2, mesh.shape["sub"]), ("slab_0", "slab_1", "slab_2", "sub")
    )
    return jax.shard_map(
        body,
        mesh=torus,
        in_specs=(
            P(None, None, None, SLAB, "sub", None),
            P(None, None, SLAB, "sub", None),
            P(None, SLAB, "sub", None),
            P(),
        ),
        out_specs=(P(None, None, SLAB, "sub", None), P(), P()),
        check_vma=False,
    )
```

profile of v0, /device:TPU:1, one launch (start us, length us, event | category | flops | bytes accessed | tf_op | source)
XLA Modules:
  0.0 146.4 jit_solution(16064751855103742166)
XLA Ops:
  0.7 0.9 fusion.73
  1.5 3.9 %collective-permute-start.2 = (f32[6,8,1,128]{3,1,2,0:T(8,128)S(1)}, f32[6,8,1,128]{3,1,2,0:T(8,128)S(1)}, u32[]{:S(2)}, u32[]{:S(2)}) collective-permute-start(f32[6,8,1,128]{3,1,2,0:T(8,128)S(1)} %get-tuple-element.108), channel_id=1, source_target_pairs={{0,1},{1,2},{2,3},{4,5},{5,6},{6,7},{8,9},{9,10},{10,11},{12,13},{... | collective-permute-start | bytes 73736 | tf_op jit(solution)/shard_map/ppermute | solution.py:18
  5.5 1.0 fusion.74
  6.5 6.1 %collective-permute-start.1 = (f32[6,1,3,128]{3,1,2,0:T(1,128)S(1)}, f32[6,1,3,128]{3,1,2,0:T(1,128)S(1)}, u32[]{:S(2)}, u32[]{:S(2)}) collective-permute-start(f32[6,1,3,128]{3,1,2,0:T(1,128)S(1)} %get-tuple-element.111), channel_id=1, source_target_pairs={{4,0},{8,4},{12,8},{16,12},{20,16},{24,20},{28,24},{32,28},{36,32}... | collective-permute-start | bytes 27656 | tf_op jit(solution)/shard_map/ppermute | solution.py:19
  12.6 1.9 %collective-permute-start = (f32[6,1,3,128]{3,1,2,0:T(1,128)S(1)}, f32[6,1,3,128]{3,1,2,0:T(1,128)S(1)}, u32[]{:S(2)}, u32[]{:S(2)}) collective-permute-start(f32[6,1,3,128]{3,1,2,0:T(1,128)S(1)} %get-tuple-element.110), channel_id=1, source_target_pairs={{0,4},{4,8},{8,12},{12,16},{16,20},{20,24},{24,28},{28,32},{32,36}... | collective-permute-start | bytes 27656 | tf_op jit(solution)/shard_map/ppermute | solution.py:18
  14.5 1.3 collective-permute-start.3
  15.8 1.0 fusion.72
  16.9 5.4 %fusion.4 = f32[30,30]{1,0:T(8,128)S(1)} fusion(f32[30,6,8,3,128]{4,2,3,1,0:T(8,128)} %param.5), kind=kOutput, calls=%fused_computation.5 | convolution fusion | flops 199065600 | bytes 2215440 | tf_op jit(solution)/shard_map/dot_general | solution.py:94
  22.3 0.7 fusion.75
  27.1 1.3 collective-permute-start.7
  28.4 2.4 %collective-permute-start.5 = (f32[6,1,3,128]{3,1,2,0:T(1,128)S(1)}, f32[6,1,3,128]{3,1,2,0:T(1,128)S(1)}, u32[]{:S(2)}, u32[]{:S(2)}) collective-permute-start(f32[6,1,3,128]{3,1,2,0:T(1,128)S(1)} %get-tuple-element.104), channel_id=1, source_target_pairs={{4,0},{8,4},{12,8},{16,12},{20,16},{24,20},{28,24},{32,28},{36,32}... | collective-permute-start | bytes 27656 | tf_op jit(solution)/shard_map/ppermute | solution.py:19
  30.8 3.2 %collective-permute-start.4 = (f32[6,1,3,128]{3,1,2,0:T(1,128)S(1)}, f32[6,1,3,128]{3,1,2,0:T(1,128)S(1)}, u32[]{:S(2)}, u32[]{:S(2)}) collective-permute-start(f32[6,1,3,128]{3,1,2,0:T(1,128)S(1)} %get-tuple-element.105), channel_id=1, source_target_pairs={{0,4},{4,8},{8,12},{12,16},{16,20},{20,24},{24,28},{28,32},{32,36}... | collective-permute-start | bytes 27656 | tf_op jit(solution)/shard_map/ppermute | solution.py:18
  34.0 4.6 %collective-permute-start.6 = (f32[6,8,1,128]{3,1,2,0:T(8,128)S(1)}, f32[6,8,1,128]{3,1,2,0:T(8,128)S(1)}, u32[]{:S(2)}, u32[]{:S(2)}) collective-permute-start(f32[6,8,1,128]{3,1,2,0:T(8,128)S(1)} %get-tuple-element.103), channel_id=1, source_target_pairs={{0,1},{1,2},{2,3},{4,5},{5,6},{6,7},{8,9},{9,10},{10,11},{12,13},{... | collective-permute-start | bytes 73736 | tf_op jit(solution)/shard_map/ppermute | solution.py:18
  38.9 0.7 collective-permute-done.6
  40.0 1.3 collective-permute-start.11
  41.3 2.3 %collective-permute-start.9 = (f32[6,1,3,128]{3,1,2,0:T(1,128)S(1)}, f32[6,1,3,128]{3,1,2,0:T(1,128)S(1)}, u32[]{:S(2)}, u32[]{:S(2)}) collective-permute-start(f32[6,1,3,128]{3,1,2,0:T(1,128)S(1)} %get-tuple-element.98), channel_id=1, source_target_pairs={{4,0},{8,4},{12,8},{16,12},{20,16},{24,20},{28,24},{32,28},{36,32}... | collective-permute-start | bytes 27656 | tf_op jit(solution)/shard_map/ppermute | solution.py:19
  43.6 3.3 %collective-permute-start.8 = (f32[6,1,3,128]{3,1,2,0:T(1,128)S(1)}, f32[6,1,3,128]{3,1,2,0:T(1,128)S(1)}, u32[]{:S(2)}, u32[]{:S(2)}) collective-permute-start(f32[6,1,3,128]{3,1,2,0:T(1,128)S(1)} %get-tuple-element.99), channel_id=1, source_target_pairs={{0,4},{4,8},{8,12},{12,16},{16,20},{20,24},{24,28},{28,32},{32,36}... | collective-permute-start | bytes 27656 | tf_op jit(solution)/shard_map/ppermute | solution.py:18
  46.9 4.7 %collective-permute-start.10 = (f32[6,8,1,128]{3,1,2,0:T(8,128)S(1)}, f32[6,8,1,128]{3,1,2,0:T(8,128)S(1)}, u32[]{:S(2)}, u32[]{:S(2)}) collective-permute-start(f32[6,8,1,128]{3,1,2,0:T(8,128)S(1)} %get-tuple-element.97), channel_id=1, source_target_pairs={{0,1},{1,2},{2,3},{4,5},{5,6},{6,7},{8,9},{9,10},{10,11},{12,13},{... | collective-permute-start | bytes 73736 | tf_op jit(solution)/shard_map/ppermute | solution.py:18
  51.8 0.7 copy.313
  53.0 1.3 collective-permute-start.15
  54.3 1.9 %collective-permute-start.13 = (f32[6,1,3,128]{3,1,2,0:T(1,128)S(1)}, f32[6,1,3,128]{3,1,2,0:T(1,128)S(1)}, u32[]{:S(2)}, u32[]{:S(2)}) collective-permute-start(f32[6,1,3,128]{3,1,2,0:T(1,128)S(1)} %get-tuple-element.92), channel_id=1, source_target_pairs={{4,0},{8,4},{12,8},{16,12},{20,16},{24,20},{28,24},{32,28},{36,32}... | collective-permute-start | bytes 27656 | tf_op jit(solution)/shard_map/ppermute | solution.py:19
  56.2 3.6 %collective-permute-start.12 = (f32[6,1,3,128]{3,1,2,0:T(1,128)S(1)}, f32[6,1,3,128]{3,1,2,0:T(1,128)S(1)}, u32[]{:S(2)}, u32[]{:S(2)}) collective-permute-start(f32[6,1,3,128]{3,1,2,0:T(1,128)S(1)} %get-tuple-element.93), channel_id=1, source_target_pairs={{0,4},{4,8},{8,12},{12,16},{16,20},{20,24},{24,28},{28,32},{32,36}... | collective-permute-start | bytes 27656 | tf_op jit(solution)/shard_map/ppermute | solution.py:18
  59.9 4.3 %collective-permute-start.14 = (f32[6,8,1,128]{3,1,2,0:T(8,128)S(1)}, f32[6,8,1,128]{3,1,2,0:T(8,128)S(1)}, u32[]{:S(2)}, u32[]{:S(2)}) collective-permute-start(f32[6,8,1,128]{3,1,2,0:T(8,128)S(1)} %get-tuple-element.91), channel_id=1, source_target_pairs={{0,1},{1,2},{2,3},{4,5},{5,6},{6,7},{8,9},{9,10},{10,11},{12,13},{... | collective-permute-start | bytes 73736 | tf_op jit(solution)/shard_map/ppermute | solution.py:18
  64.4 0.7 copy.314
  65.5 1.3 collective-permute-start.19
  66.8 1.9 %collective-permute-start.17 = (f32[6,1,3,128]{3,1,2,0:T(1,128)S(1)}, f32[6,1,3,128]{3,1,2,0:T(1,128)S(1)}, u32[]{:S(2)}, u32[]{:S(2)}) collective-permute-start(f32[6,1,3,128]{3,1,2,0:T(1,128)S(1)} %get-tuple-element.86), channel_id=1, source_target_pairs={{4,0},{8,4},{12,8},{16,12},{20,16},{24,20},{28,24},{32,28},{36,32}... | collective-permute-start | bytes 27656 | tf_op jit(solution)/shard_map/ppermute | solution.py:19
  68.8 3.6 %collective-permute-start.16 = (f32[6,1,3,128]{3,1,2,0:T(1,128)S(1)}, f32[6,1,3,128]{3,1,2,0:T(1,128)S(1)}, u32[]{:S(2)}, u32[]{:S(2)}) collective-permute-start(f32[6,1,3,128]{3,1,2,0:T(1,128)S(1)} %get-tuple-element.87), channel_id=1, source_target_pairs={{0,4},{4,8},{8,12},{12,16},{16,20},{20,24},{24,28},{28,32},{32,36}... | collective-permute-start | bytes 27656 | tf_op jit(solution)/shard_map/ppermute | solution.py:18
  72.4 4.3 %collective-permute-start.18 = (f32[6,8,1,128]{3,1,2,0:T(8,128)S(1)}, f32[6,8,1,128]{3,1,2,0:T(8,128)S(1)}, u32[]{:S(2)}, u32[]{:S(2)}) collective-permute-start(f32[6,8,1,128]{3,1,2,0:T(8,128)S(1)} %get-tuple-element.85), channel_id=1, source_target_pairs={{0,1},{1,2},{2,3},{4,5},{5,6},{6,7},{8,9},{9,10},{10,11},{12,13},{... | collective-permute-start | bytes 73736 | tf_op jit(solution)/shard_map/ppermute | solution.py:18
  77.1 0.6 collective-permute-done.18
  78.2 0.7 stack.41
  79.0 4.0 %fusion.7 = f32[30,6]{0,1:T(8,128)S(1)} fusion(f32[6,6,8,3,128]{4,0,3,2,1:T(8,128)S(1)} %stack.41, f32[30,6,8,3,128]{4,2,3,1,0:T(8,128)} %param.5), kind=kOutput, calls=%fused_computation.6 | convolution fusion | flops 39813120 | bytes 2654928 | tf_op jit(solution)/shard_map/dot_general | solution.py:92
  82.9 1.4 convolution_bitcast_fusion
  84.8 10.9 %all_to_all.12 = f32[8,1,1116]{2,1,0:T(1,128)S(1)} all-to-all(f32[8,1,1116]{2,1,0:T(1,128)S(1)} %broadcast_in_dim.5), channel_id=1, replica_groups=mesh['slab_0'=4,'slab_1'=16,'slab_2'=2,'sub'=4] {'slab_2','sub'}, dimensions={0} | all-to-all | bytes 71424 | tf_op jit(solution)/shard_map/all_to_all | solution.py:32
  95.7 0.9 broadcast_in_dim.6
  96.6 20.9 %all-to-all-start.1 = ((f32[64,1,1116]{2,1,0:T(1,128)}), f32[64,1,1116]{2,1,0:T(1,128)S(1)}, u32[]{:S(2)}, u32[]{:S(2)}) async-start(f32[64,1,1116]{2,1,0:T(1,128)} %broadcast_in_dim.6), calls=%async_computation.1 | async-start | bytes 589824 | tf_op jit(solution)/shard_map/all_to_all | solution.py:32
  117.5 2.5 %copy.334 = f32[30,6,8,3,128]{4,3,2,1,0:T(4,128)} copy(f32[30,6,8,3,128]{4,2,3,1,0:T(8,128)S(1)} %copy-done.1) | data formatting | bytes 4423680 | tf_op args[1]
  120.1 3.3 %reshape.153 = f32[30,18432]{1,0:T(8,128)S(1)} reshape(f32[30,6,8,3,128]{4,3,2,1,0:T(4,128)} %copy.334) | data formatting | bytes 4423680 | tf_op jit(solution)/shard_map/reshape | solution.py:90
  123.4 0.7 stack.43
  124.1 0.7 stack.44
  125.2 2.0 %stack.48 = f32[6,18432]{1,0:T(8,128)S(1)} concatenate(f32[1,18432]{1,0:T(1,128)S(1)} %stack.42, f32[1,18432]{1,0:T(1,128)} %stack.43, f32[1,18432]{1,0:T(1,128)} %stack.44, f32[1,18432]{1,0:T(1,128)S(1)} %stack.45, f32[1,18432]{1,0:T(1,128)S(1)} %stack.46, f32[1,18432]{1,0:T(1,128)S(1)} %stack.47), dimensions={0} | concatenate | bytes 884736 | tf_op jit(solution)/shard_map/stack | solution.py:87
  127.2 11.3 %all-to-all-done.1 = f32[64,1,1116]{2,1,0:T(1,128)S(1)} async-done(((f32[64,1,1116]{2,1,0:T(1,128)}), f32[64,1,1116]{2,1,0:T(1,128)S(1)}, u32[]{:S(2)}, u32[]{:S(2)}) %all-to-all-start.1) | async-done | bytes 285728 | tf_op jit(solution)/shard_map/all_to_all | solution.py:32
  139.1 0.7 copy.337
  141.1 0.6 compare_reduce_fusion
  141.8 0.6 fusion.59
  142.9 1.2 convolution_subtract_fusion
  144.2 0.8 fusion.56
  144.9 0.8 copy.336
  145.8 0.7 copy.338
  (104 shorter events, 6.8 us)
Async XLA Ops:
  0.6 25.7 %copy-start.2 = (f32[6,8,3,128]{3,1,2,0:T(8,128)S(1)}, f32[6,8,3,128]{3,1,2,0:T(8,128)}, u32[]{:S(2)}) copy-start(f32[6,8,3,128]{3,1,2,0:T(8,128)} %param.6) | copy-start | bytes 221188
  0.6 21.7 %copy-start.5 = (f32[5]{0:T(128)S(1)}, f32[5]{0:T(128)}, u32[]{:S(2)}) copy-start(f32[5]{0:T(128)} %param.7) | copy-start | bytes 64
  0.7 26.0 %copy-start = (bf16[7,6,6,8,3,128]{5,3,4,2,1,0:T(8,128)(2,1)S(1)}, bf16[7,6,6,8,3,128]{5,3,4,2,1,0:T(8,128)(2,1)}, u32[]{:S(2)}) copy-start(bf16[7,6,6,8,3,128]{5,3,4,2,1,0:T(8,128)(2,1)} %param.4) | copy-start | bytes 4644868
  1.5 25.1 %collective-permute-start.2 = (f32[6,8,1,128]{3,1,2,0:T(8,128)S(1)}, f32[6,8,1,128]{3,1,2,0:T(8,128)S(1)}, u32[]{:S(2)}, u32[]{:S(2)}) collective-permute-start(f32[6,8,1,128]{3,1,2,0:T(8,128)S(1)} %get-tuple-element.108), channel_id=1, source_target_pairs={{0,1},{1,2},{2,3},{4,5},{5,6},{6,7},{8,9},{9,10},{10,11},{12,13},{... | collective-permute-start | bytes 73736 | tf_op jit(solution)/shard_map/ppermute | solution.py:18
  6.5 20.1 %collective-permute-start.1 = (f32[6,1,3,128]{3,1,2,0:T(1,128)S(1)}, f32[6,1,3,128]{3,1,2,0:T(1,128)S(1)}, u32[]{:S(2)}, u32[]{:S(2)}) collective-permute-start(f32[6,1,3,128]{3,1,2,0:T(1,128)S(1)} %get-tuple-element.111), channel_id=1, source_target_pairs={{4,0},{8,4},{12,8},{16,12},{20,16},{24,20},{28,24},{32,28},{36,32}... | collective-permute-start | bytes 27656 | tf_op jit(solution)/shard_map/ppermute | solution.py:19
  12.6 14.0 %collective-permute-start = (f32[6,1,3,128]{3,1,2,0:T(1,128)S(1)}, f32[6,1,3,128]{3,1,2,0:T(1,128)S(1)}, u32[]{:S(2)}, u32[]{:S(2)}) collective-permute-start(f32[6,1,3,128]{3,1,2,0:T(1,128)S(1)} %get-tuple-element.110), channel_id=1, source_target_pairs={{0,4},{4,8},{8,12},{12,16},{16,20},{20,24},{24,28},{28,32},{32,36}... | collective-permute-start | bytes 27656 | tf_op jit(solution)/shard_map/ppermute | solution.py:18
  14.5 12.1 %collective-permute-start.3 = (f32[6,8,1,128]{3,1,2,0:T(8,128)S(1)}, f32[6,8,1,128]{3,1,2,0:T(8,128)S(1)}, u32[]{:S(2)}, u32[]{:S(2)}) collective-permute-start(f32[6,8,1,128]{3,1,2,0:T(8,128)S(1)} %get-tuple-element.109), channel_id=1, source_target_pairs={{1,0},{2,1},{3,2},{5,4},{6,5},{7,6},{9,8},{10,9},{11,10},{13,12},{... | collective-permute-start | bytes 73736 | tf_op jit(solution)/shard_map/ppermute | solution.py:19
  27.1 11.8 %collective-permute-start.7 = (f32[6,8,1,128]{3,1,2,0:T(8,128)S(1)}, f32[6,8,1,128]{3,1,2,0:T(8,128)S(1)}, u32[]{:S(2)}, u32[]{:S(2)}) collective-permute-start(f32[6,8,1,128]{3,1,2,0:T(8,128)S(1)} %get-tuple-element.102), channel_id=1, source_target_pairs={{1,0},{2,1},{3,2},{5,4},{6,5},{7,6},{9,8},{10,9},{11,10},{13,12},{... | collective-permute-start | bytes 73736 | tf_op jit(solution)/shard_map/ppermute | solution.py:19
  28.4 10.5 %collective-permute-start.5 = (f32[6,1,3,128]{3,1,2,0:T(1,128)S(1)}, f32[6,1,3,128]{3,1,2,0:T(1,128)S(1)}, u32[]{:S(2)}, u32[]{:S(2)}) collective-permute-start(f32[6,1,3,128]{3,1,2,0:T(1,128)S(1)} %get-tuple-element.104), channel_id=1, source_target_pairs={{4,0},{8,4},{12,8},{16,12},{20,16},{24,20},{28,24},{32,28},{36,32}... | collective-permute-start | bytes 27656 | tf_op jit(solution)/shard_map/ppermute | solution.py:19
  30.8 8.1 %collective-permute-start.4 = (f32[6,1,3,128]{3,1,2,0:T(1,128)S(1)}, f32[6,1,3,128]{3,1,2,0:T(1,128)S(1)}, u32[]{:S(2)}, u32[]{:S(2)}) collective-permute-start(f32[6,1,3,128]{3,1,2,0:T(1,128)S(1)} %get-tuple-element.105), channel_id=1, source_target_pairs={{0,4},{4,8},{8,12},{12,16},{16,20},{20,24},{24,28},{28,32},{32,36}... | collective-permute-start | bytes 27656 | tf_op jit(solution)/shard_map/ppermute | solution.py:18
  34.0 5.6 %collective-permute-start.6 = (f32[6,8,1,128]{3,1,2,0:T(8,128)S(1)}, f32[6,8,1,128]{3,1,2,0:T(8,128)S(1)}, u32[]{:S(2)}, u32[]{:S(2)}) collective-permute-start(f32[6,8,1,128]{3,1,2,0:T(8,128)S(1)} %get-tuple-element.103), channel_id=1, source_target_pairs={{0,1},{1,2},{2,3},{4,5},{5,6},{6,7},{8,9},{9,10},{10,11},{12,13},{... | collective-permute-start | bytes 73736 | tf_op jit(solution)/shard_map/ppermute | solution.py:18
  40.0 12.5 %collective-permute-start.11 = (f32[6,8,1,128]{3,1,2,0:T(8,128)S(1)}, f32[6,8,1,128]{3,1,2,0:T(8,128)S(1)}, u32[]{:S(2)}, u32[]{:S(2)}) collective-permute-start(f32[6,8,1,128]{3,1,2,0:T(8,128)S(1)} %get-tuple-element.96), channel_id=1, source_target_pairs={{1,0},{2,1},{3,2},{5,4},{6,5},{7,6},{9,8},{10,9},{11,10},{13,12},{... | collective-permute-start | bytes 73736 | tf_op jit(solution)/shard_map/ppermute | solution.py:19
  41.3 11.2 %collective-permute-start.9 = (f32[6,1,3,128]{3,1,2,0:T(1,128)S(1)}, f32[6,1,3,128]{3,1,2,0:T(1,128)S(1)}, u32[]{:S(2)}, u32[]{:S(2)}) collective-permute-start(f32[6,1,3,128]{3,1,2,0:T(1,128)S(1)} %get-tuple-element.98), channel_id=1, source_target_pairs={{4,0},{8,4},{12,8},{16,12},{20,16},{24,20},{28,24},{32,28},{36,32}... | collective-permute-start | bytes 27656 | tf_op jit(solution)/shard_map/ppermute | solution.py:19
  43.6 8.9 %collective-permute-start.8 = (f32[6,1,3,128]{3,1,2,0:T(1,128)S(1)}, f32[6,1,3,128]{3,1,2,0:T(1,128)S(1)}, u32[]{:S(2)}, u32[]{:S(2)}) collective-permute-start(f32[6,1,3,128]{3,1,2,0:T(1,128)S(1)} %get-tuple-element.99), channel_id=1, source_target_pairs={{0,4},{4,8},{8,12},{12,16},{16,20},{20,24},{24,28},{28,32},{32,36}... | collective-permute-start | bytes 27656 | tf_op jit(solution)/shard_map/ppermute | solution.py:18
  46.9 5.7 %collective-permute-start.10 = (f32[6,8,1,128]{3,1,2,0:T(8,128)S(1)}, f32[6,8,1,128]{3,1,2,0:T(8,128)S(1)}, u32[]{:S(2)}, u32[]{:S(2)}) collective-permute-start(f32[6,8,1,128]{3,1,2,0:T(8,128)S(1)} %get-tuple-element.97), channel_id=1, source_target_pairs={{0,1},{1,2},{2,3},{4,5},{5,6},{6,7},{8,9},{9,10},{10,11},{12,13},{... | collective-permute-start | bytes 73736 | tf_op jit(solution)/shard_map/ppermute | solution.py:18
  53.0 12.1 %collective-permute-start.15 = (f32[6,8,1,128]{3,1,2,0:T(8,128)S(1)}, f32[6,8,1,128]{3,1,2,0:T(8,128)S(1)}, u32[]{:S(2)}, u32[]{:S(2)}) collective-permute-start(f32[6,8,1,128]{3,1,2,0:T(8,128)S(1)} %get-tuple-element.90), channel_id=1, source_target_pairs={{1,0},{2,1},{3,2},{5,4},{6,5},{7,6},{9,8},{10,9},{11,10},{13,12},{... | collective-permute-start | bytes 73736 | tf_op jit(solution)/shard_map/ppermute | solution.py:19
  54.3 10.7 %collective-permute-start.13 = (f32[6,1,3,128]{3,1,2,0:T(1,128)S(1)}, f32[6,1,3,128]{3,1,2,0:T(1,128)S(1)}, u32[]{:S(2)}, u32[]{:S(2)}) collective-permute-start(f32[6,1,3,128]{3,1,2,0:T(1,128)S(1)} %get-tuple-element.92), channel_id=1, source_target_pairs={{4,0},{8,4},{12,8},{16,12},{20,16},{24,20},{28,24},{32,28},{36,32}... | collective-permute-start | bytes 27656 | tf_op jit(solution)/shard_map/ppermute | solution.py:19
  56.2 8.8 %collective-permute-start.12 = (f32[6,1,3,128]{3,1,2,0:T(1,128)S(1)}, f32[6,1,3,128]{3,1,2,0:T(1,128)S(1)}, u32[]{:S(2)}, u32[]{:S(2)}) collective-permute-start(f32[6,1,3,128]{3,1,2,0:T(1,128)S(1)} %get-tuple-element.93), channel_id=1, source_target_pairs={{0,4},{4,8},{8,12},{12,16},{16,20},{20,24},{24,28},{28,32},{32,36}... | collective-permute-start | bytes 27656 | tf_op jit(solution)/shard_map/ppermute | solution.py:18
  59.9 5.2 %collective-permute-start.14 = (f32[6,8,1,128]{3,1,2,0:T(8,128)S(1)}, f32[6,8,1,128]{3,1,2,0:T(8,128)S(1)}, u32[]{:S(2)}, u32[]{:S(2)}) collective-permute-start(f32[6,8,1,128]{3,1,2,0:T(8,128)S(1)} %get-tuple-element.91), channel_id=1, source_target_pairs={{0,1},{1,2},{2,3},{4,5},{5,6},{6,7},{8,9},{9,10},{10,11},{12,13},{... | collective-permute-start | bytes 73736 | tf_op jit(solution)/shard_map/ppermute | solution.py:18
  65.5 11.5 %collective-permute-start.19 = (f32[6,8,1,128]{3,1,2,0:T(8,128)S(1)}, f32[6,8,1,128]{3,1,2,0:T(8,128)S(1)}, u32[]{:S(2)}, u32[]{:S(2)}) collective-permute-start(f32[6,8,1,128]{3,1,2,0:T(8,128)S(1)} %get-tuple-element.84), channel_id=1, source_target_pairs={{1,0},{2,1},{3,2},{5,4},{6,5},{7,6},{9,8},{10,9},{11,10},{13,12},{... | collective-permute-start | bytes 73736 | tf_op jit(solution)/shard_map/ppermute | solution.py:19
  66.8 10.2 %collective-permute-start.17 = (f32[6,1,3,128]{3,1,2,0:T(1,128)S(1)}, f32[6,1,3,128]{3,1,2,0:T(1,128)S(1)}, u32[]{:S(2)}, u32[]{:S(2)}) collective-permute-start(f32[6,1,3,128]{3,1,2,0:T(1,128)S(1)} %get-tuple-element.86), channel_id=1, source_target_pairs={{4,0},{8,4},{12,8},{16,12},{20,16},{24,20},{28,24},{32,28},{36,32}... | collective-permute-start | bytes 27656 | tf_op jit(solution)/shard_map/ppermute | solution.py:19
  68.8 8.3 %collective-permute-start.16 = (f32[6,1,3,128]{3,1,2,0:T(1,128)S(1)}, f32[6,1,3,128]{3,1,2,0:T(1,128)S(1)}, u32[]{:S(2)}, u32[]{:S(2)}) collective-permute-start(f32[6,1,3,128]{3,1,2,0:T(1,128)S(1)} %get-tuple-element.87), channel_id=1, source_target_pairs={{0,4},{4,8},{8,12},{12,16},{16,20},{20,24},{24,28},{28,32},{32,36}... | collective-permute-start | bytes 27656 | tf_op jit(solution)/shard_map/ppermute | solution.py:18
  72.4 5.3 %collective-permute-start.18 = (f32[6,8,1,128]{3,1,2,0:T(8,128)S(1)}, f32[6,8,1,128]{3,1,2,0:T(8,128)S(1)}, u32[]{:S(2)}, u32[]{:S(2)}) collective-permute-start(f32[6,8,1,128]{3,1,2,0:T(8,128)S(1)} %get-tuple-element.85), channel_id=1, source_target_pairs={{0,1},{1,2},{2,3},{4,5},{5,6},{6,7},{8,9},{9,10},{10,11},{12,13},{... | collective-permute-start | bytes 73736 | tf_op jit(solution)/shard_map/ppermute | solution.py:18
  76.8 1.3 copy-start.3
  76.8 1.3 copy-start.4
  78.9 38.5 %copy-start.1 = (f32[30,6,8,3,128]{4,2,3,1,0:T(8,128)S(1)}, f32[30,6,8,3,128]{4,2,3,1,0:T(8,128)}, u32[]{:S(2)}) copy-start(f32[30,6,8,3,128]{4,2,3,1,0:T(8,128)} %param.5) | copy-start | bytes 6635524
  96.6 41.9 %all-to-all-start.1 = ((f32[64,1,1116]{2,1,0:T(1,128)}), f32[64,1,1116]{2,1,0:T(1,128)S(1)}, u32[]{:S(2)}, u32[]{:S(2)}) async-start(f32[64,1,1116]{2,1,0:T(1,128)} %broadcast_in_dim.6), calls=%async_computation.1 | async-start | bytes 589824 | tf_op jit(solution)/shard_map/all_to_all | solution.py:32
where the time goes:
time: 148 us; the launch traced here: 146 us
  starting transfers between devices  79.5 us (54%)
  local copies, waits for them, and re-layouts  20.6 us (14%)
  matrix products  13.4 us (9%)
  waiting for transfers between devices  12.7 us (9%)
  blocking collectives  10.9 us (7%)
  other arithmetic  4.78 us (3%)
  between operations  4.61 us (3%)
    ppermute x10, starting transfers between devices, padded_2(): lax.ppermute(last, axis, up)  37.5 us
    ppermute x10, starting transfers between devices, padded_2(): lax.ppermute(first, axis, [(b, a) for a, b in up])  21.1 us
    all_to_all x1, starting transfers between devices, copy_for_each(): return lax.all_to_all(copies, axis, split_axis=0, concat_axis=0, tiled=True)  20.9 us
    all_to_all x1, waiting for transfers between devices, copy_for_each(): return lax.all_to_all(copies, axis, split_axis=0, concat_axis=0, tiled=True)  11.3 us
    all_to_all x1, blocking collectives, copy_for_each(): return lax.all_to_all(copies, axis, split_axis=0, concat_axis=0, tiled=True)  10.9 us
    another operation x14, local copies, waits for them, and re-layouts, body(): basis = jnp.stack(vectors)  6.2 us
    dot_general x1, matrix products, body(): jnp.dot(earlier_flat, earlier_flat.T, precision=lax.Precision.HIGHEST)  5.43 us
    unnamed x17, local copies, waits for them, and re-layouts  4.74 us
  transfers between devices with their start and end apart: 21, of which 3 were waited for; matrix products, arithmetic and copies ran while one was open for 14% of the time, Pallas kernels for 0%

commit v1 on v0

v1 whole, which is shorter than its diff:
```python
import jax
import jax.numpy as jnp
from jax import lax
from jax.experimental import pallas as pl
from jax.experimental.pallas import tpu as pltpu
from jax.sharding import Mesh
from jax.sharding import PartitionSpec as P

SLAB = ("slab_0", "slab_1", "slab_2")
NEAR = ("slab_0", "slab_2", "sub")
FAR = ("slab_1",)
EXACT = lax.Precision.HIGHEST


def chain(count):
    up = [(i, i + 1) for i in range(count - 1)]
    return up, [(b, a) for a, b in up]


def over_copies(x, axis):
    copies = jnp.broadcast_to(x, (lax.axis_size(axis), *x.shape))
    everything = lax.all_to_all(copies, axis, split_axis=0, concat_axis=0, tiled=True)
    return jnp.sum(everything, axis=0)


def packed_total(arrays):
    ravelled, at, done = (jnp.concatenate([a.reshape(-1) for a in arrays]), 0, [])
    so_far = over_copies(over_copies(ravelled[None], NEAR), FAR)[0]
    for a in arrays:
        done.append(so_far[at : at + a.size].reshape(a.shape))
        at += a.size
    return tuple(done)


def swap_halves(x):
    return pltpu.roll(x, x.shape[0] // 2, 0)


def half_mask(shape):
    return lax.broadcasted_iota(jnp.int32, shape, len(shape) - 2) < shape[-2] // 2


def pack(c_ref, s_ref, own_ref, lo_ref, hi_ref, start_ref, sems):
    parts = sems.shape[0]
    size = c_ref.shape[0] // parts
    copies = [
        pltpu.make_async_copy(
            c_ref.at[pl.ds(n * size, size)], own_ref.at[pl.ds(n * size, size)], sems.at[n]
        )
        for n in range(parts)
    ]
    for copy in copies:
        copy.start()
    start_ref[...] = s_ref[...]
    first = half_mask(c_ref.shape[2:])

    def pair(p, carry):
        a, b = own_ref[p, 0].astype(jnp.float32), own_ref[p, 1].astype(jnp.float32)
        hi_ref[p] = jnp.where(first, a, swap_halves(b)).astype(hi_ref.dtype)
        lo_ref[p] = jnp.where(first, swap_halves(a), b).astype(lo_ref.dtype)
        return carry

    for n, copy in enumerate(copies):
        copy.wait()
        lax.fori_loop(n * size, (n + 1) * size, pair, 0, unroll=9)


def unpack(lo_ref, hi_ref, wide_ref):
    first = half_mask(lo_ref.shape[1:])

    def pair(p, carry):
        lo, hi = lo_ref[p].astype(jnp.float32), hi_ref[p].astype(jnp.float32)
        wide_ref[p, 0] = jnp.where(first, hi, swap_halves(lo)).astype(wide_ref.dtype)
        wide_ref[p, 1] = jnp.where(first, swap_halves(hi), lo).astype(wide_ref.dtype)
        return carry

    lax.fori_loop(0, lo_ref.shape[0], pair, 0, unroll=9)


def in_vmem(x):
    return pltpu.with_memory_space_constraint(x, pltpu.VMEM)


def in_hbm(x):
    return pltpu.with_memory_space_constraint(x, pltpu.HBM)


VMEM = pl.BlockSpec(memory_space=pltpu.VMEM)
ANY = pl.BlockSpec(memory_space=pl.ANY)
SMEM = pl.BlockSpec(memory_space=pltpu.SMEM)
LIMIT = pltpu.CompilerParams(vmem_limit_bytes=2 * 2**20)


def cost(flops, size):
    return pl.CostEstimate(flops=flops, bytes_accessed=size, transcendentals=0)


def packed(coefficients, start):
    pairs = coefficients.reshape(-1, 2, *coefficients.shape[-2:])
    half = pltpu.VMEM((pairs.shape[0], *pairs.shape[2:]), pairs.dtype)
    return pl.pallas_call(
        pack,
        out_shape=(
            pltpu.VMEM(pairs.shape, pairs.dtype), half, half, pltpu.VMEM(start.shape, start.dtype)
        ),
        in_specs=[pl.BlockSpec(memory_space=pltpu.HBM), VMEM],
        out_specs=(VMEM,) * 4,
        scratch_shapes=[pltpu.SemaphoreType.DMA((6,))],
        compiler_params=LIMIT,
        cost_estimate=cost(10**6, 4 * 10**6),
    )(in_hbm(pairs), in_vmem(start))


def unpacked(lo, hi):
    return pl.pallas_call(
        unpack,
        out_shape=pltpu.VMEM((lo.shape[0], 2, *lo.shape[1:]), lo.dtype),
        in_specs=[VMEM] * 2,
        out_specs=VMEM,
        compiler_params=LIMIT,
        cost_estimate=cost(10**6, 4 * 10**6),
    )(in_vmem(lo), in_vmem(hi))


def is_odd():
    return lax.rem(lax.axis_index("sub"), 2) > 0


def begin_kernel(s_ref, lo_ref, hi_ref, v_ref, one_ref, two_ref):
    columns = s_ref.shape[1]
    v_ref[0] = s_ref[...]
    v_ref[1] = jnp.where(half_mask(s_ref.shape), hi_ref[...], lo_ref[...])
    odd = is_odd()
    near, far = v_ref[:, :, 0], v_ref[:, :, columns - 1]
    one_ref[...] = jnp.where(odd, near, far)
    two_ref[...] = jnp.where(odd, far, near)


def begun(start, s_lo, s_hi):
    edge = pltpu.VMEM((2, start.shape[0], *start.shape[2:]), start.dtype)
    return pl.pallas_call(
        begin_kernel,
        out_shape=(pltpu.VMEM((2, *start.shape), start.dtype), edge, edge),
        in_specs=[VMEM] * 3,
        out_specs=(VMEM,) * 3,
        compiler_params=LIMIT,
        cost_estimate=cost(10**5, 10**5),
    )(*(in_vmem(x) for x in (start, s_lo, s_hi)))


def early_kernel(e_ref, s_ref, held_ref, start_ref, sem):
    copy = pltpu.make_async_copy(e_ref, held_ref, sem.at[0])
    copy.start()
    start_ref[...] = s_ref[...]
    copy.wait()


def held(earlier, start):
    return pl.pallas_call(
        early_kernel,
        out_shape=(pltpu.VMEM(earlier.shape, earlier.dtype), pltpu.VMEM(start.shape, start.dtype)),
        in_specs=[pl.BlockSpec(memory_space=pltpu.HBM), VMEM],
        out_specs=(VMEM,) * 2,
        scratch_shapes=[pltpu.SemaphoreType.DMA((1,))],
        compiler_params=LIMIT,
        cost_estimate=cost(10**5, 5 * 10**6),
    )(in_hbm(earlier), in_vmem(start))


def step_kernel(step, first_step, last_step, shifts_ref, *refs):
    split = len(refs) - (1 if last_step else 3)
    (own_ref, wide_ref, v_ref, one_ref, two_ref, *more), outs = refs[:split], refs[split:]
    odd = is_odd()
    comps, columns = v_ref.shape[1:3]
    rows, lanes = v_ref.shape[3:]
    keep = 1.0 - shifts_ref[step]
    row = lax.broadcasted_iota(jnp.int32, (rows, lanes), 0)
    lane = lax.broadcasted_iota(jnp.int32, (rows, lanes), 1)
    for x in range(columns):
        acc = [[None] * comps for _ in range(1 if last_step else 2)]
        for e in range(comps):
            own, ext = v_ref[0, e, x], v_ref[1, e, x]
            down, up = pltpu.roll(own, 1, 0), pltpu.roll(own, rows - 1, 0)
            ext_down, ext_up = pltpu.roll(ext, 1, 0), pltpu.roll(ext, rows - 1, 0)
            if first_step:
                lo, hi = more[0][e, x], more[1][e, x]
                low = row < rows // 2
                wide_down = jnp.where(low, pltpu.roll(hi, 1, 0), pltpu.roll(lo, 1, 0))
                wide_up = jnp.where(low, pltpu.roll(hi, rows - 1, 0), pltpu.roll(lo, rows - 1, 0))
            else:
                wide_down, wide_up = ext_down, ext_up
            below = [jnp.where(row == 0, ext_down, down), jnp.where(row == 0, down, wide_down)]
            above = [
                jnp.where(row == rows - 1, ext_up, up),
                jnp.where(row == rows - 1, up, wide_up),
            ]
            for t, source in enumerate((own_ref, wide_ref)[: len(acc)]):
                center = v_ref[t, e, x]
                fields = [
                    center,
                    below[t],
                    above[t],
                    jnp.where(odd, one_ref[t, e], two_ref[t, e]) if x == 0 else v_ref[t, e, x - 1],
                    jnp.where(odd, two_ref[t, e], one_ref[t, e])
                    if x == columns - 1
                    else v_ref[t, e, x + 1],
                    jnp.where(lane == 0, 0.0, pltpu.roll(center, 1, 1)),
                    jnp.where(lane == lanes - 1, 0.0, pltpu.roll(center, lanes - 1, 1)),
                ]
                for c in range(comps):
                    total = acc[t][c]
                    for d, f in enumerate(fields):
                        term = source[d, c, e, x].astype(jnp.float32) * f
                        total = term if total is None else total + term
                    acc[t][c] = total
        for t in range(len(acc)):
            for c in range(comps):
                value = acc[t][c] + keep * v_ref[t, c, x]
                if last_step:
                    outs[0][c, x] = value
                else:
                    outs[0][t, c, x] = value
    if not last_step:
        for t in range(2):
            for c in range(comps):
                near, far = outs[0][t, c, 0], outs[0][t, c, columns - 1]
                outs[1][t, c] = jnp.where(odd, near, far)
                outs[2][t, c] = jnp.where(odd, far, near)


def stepped(step, depth, shifts, own, wide, v, one, two, more, after):
    last = step == depth - 1
    full = pltpu.VMEM(v.shape[1:] if last else v.shape, v.dtype)
    edge = pltpu.VMEM(one.shape, one.dtype)
    return pl.pallas_call(
        lambda *refs: step_kernel(
            step, step == 0, last, *refs[: 6 + len(more)], *refs[6 + len(more) + len(after) :]
        ),
        out_shape=(full,) if last else (full, edge, edge),
        in_specs=[SMEM] + [VMEM] * (5 + len(more)) + [ANY] * len(after),
        out_specs=(VMEM,) if last else (VMEM,) * 3,
        compiler_params=LIMIT,
        cost_estimate=cost(10**7, 3 * 10**6),
    )(shifts, *(in_vmem(a) for a in (own, wide, v, one, two, *more)), *after)


def dots_kernel(e_ref, *refs):
    *w_refs, out_ref, part = refs
    count, comps, columns = e_ref.shape[:3]
    v_ref = w_refs[-1]
    part[...] = jnp.zeros_like(part)
    group = 6
    terms = [(e_ref, j) for j in range(count)] + [(w, None) for w in w_refs]
    for at in range(0, len(terms), group):
        some = terms[at : at + group]
        acc = [None] * len(some)
        for c in range(comps):
            for x in range(columns):
                v = v_ref[c, x]
                for n, (ref, j) in enumerate(some):
                    term = v * (ref[c, x] if j is None else ref[j, c, x])
                    acc[n] = term if acc[n] is None else acc[n] + term
        for n, total in enumerate(acc):
            part[at + n : at + n + 1] = jnp.sum(total, axis=0, keepdims=True)
    ones = jnp.ones((8, part.shape[1]), jnp.float32)
    out_ref[...] = lax.dot_general(
        ones, part[...], (((1,), (1,)), ((), ())), precision=EXACT,
        preferred_element_type=jnp.float32,
    )[:1]


def dots(earlier, vectors):
    width = 40
    return pl.pallas_call(
        dots_kernel,
        out_shape=pltpu.VMEM((1, width), jnp.float32),
        in_specs=[VMEM] * (1 + len(vectors)),
        out_specs=VMEM,
        scratch_shapes=[pltpu.VMEM((width, vectors[0].shape[-1]), jnp.float32)],
        compiler_params=LIMIT,
        cost_estimate=cost(10**6, 3 * 10**6),
    )(in_vmem(earlier), *(in_vmem(v) for v in vectors))


def finish(cross_ref, turned_ref, self_ref, early_ref, e_ref, *refs):
    block = self_ref.shape[0]
    w_refs, (out_ref, proj_ref, tri_ref, o_vmem, small, spread, sems) = refs[:block], refs[block:]
    count = cross_ref.shape[0]
    p = cross_ref[...]
    proj = pltpu.make_async_copy(turned_ref, proj_ref, sems.at[0])
    proj.start()
    part = jnp.dot(early_ref[...], p, precision=EXACT) - 2.0 * p
    gram = self_ref[...] + jnp.dot(turned_ref[...], part, precision=EXACT)
    row = lax.broadcasted_iota(jnp.int32, (block, block), 0)
    col = lax.broadcasted_iota(jnp.int32, (block, block), 1)
    unit = jnp.where(row == col, 1.0, 0.0)
    a = jnp.concatenate([gram, unit, -turned_ref[...]], axis=1)
    rows = lax.broadcasted_iota(jnp.int32, a.shape, 0)
    for k in range(block):
        scale = 1.0 / jnp.sqrt(a[k : k + 1, k : k + 1])
        pivot = a[k : k + 1] * scale
        factor = a[:, k : k + 1] * scale
        a = jnp.where(rows == k, pivot, jnp.where(rows > k, a - factor * pivot, a))
    small[...] = jnp.where(row <= col, a[:, :block], 0.0)
    tri = pltpu.make_async_copy(small, tri_ref, sems.at[1])
    tri.start()
    shape = spread.shape[2:]
    for k in range(block):
        for i in range(block + count):
            if i >= block or i <= k:
                at = block + i
                spread[i, k] = jnp.broadcast_to(a[k : k + 1, at : at + 1], shape)
    outs = []
    comps = 2
    for g in range(e_ref.shape[1] // comps):
        sel = slice(g * comps, (g + 1) * comps)
        acc = [None] * block
        for i in range(block + count):
            x = w_refs[i][sel] if i < block else e_ref[i - block, sel]
            for k in range(block):
                if i >= block or i <= k:
                    t = spread[i, k][None, None] * x
                    acc[k] = t if acc[k] is None else acc[k] + t
        for k in range(block):
            o_vmem[g, k] = acc[k]
        c = pltpu.make_async_copy(o_vmem.at[g], out_ref.at[:, sel], sems.at[2 + g])
        c.start()
        outs.append(c)
    for c in [proj, tri, *outs]:
        c.wait()


def finished(cross, turned, self_sum, early, vectors, earlier):
    block = len(vectors)
    fields, *rest = vectors[0].shape
    return pl.pallas_call(
        finish,
        out_shape=(
            pltpu.HBM((block, fields, *rest), jnp.float32),
            pltpu.HBM(turned.shape, jnp.float32),
            pltpu.HBM(self_sum.shape, jnp.float32),
        ),
        in_specs=[VMEM] * (5 + block),
        out_specs=(pl.BlockSpec(memory_space=pltpu.HBM),) * 3,
        scratch_shapes=[
            pltpu.VMEM((fields // 2, block, 2, *rest), jnp.float32),
            pltpu.VMEM(self_sum.shape, jnp.float32),
            pltpu.VMEM((block + earlier.shape[0], block, *rest[1:]), jnp.float32),
            pltpu.SemaphoreType.DMA((2 + fields // 2,)),
        ],
        compiler_params=LIMIT,
        cost_estimate=cost(10**7, 3 * 10**6),
    )(*(in_vmem(x) for x in (cross, turned, self_sum, early, earlier, *vectors)))


def body(coefficients, earlier, start, shifts):
    depth = shifts.shape[0]
    coefficients = jnp.transpose(coefficients, (0, 1, 2, 4, 3, 5))
    earlier = jnp.transpose(earlier, (0, 1, 3, 2, 4))
    start = jnp.transpose(start, (0, 2, 1, 3))
    up, down = chain(lax.axis_size(SLAB))
    columns = lax.axis_size("sub")
    pairs = [(i, i ^ 1) for i in range(columns)]
    between = [(i, ((i + 1) ^ 1) - 1) for i in range(1, columns - 1)]
    own, lo, hi, start = packed(coefficients, start)
    lo = lax.ppermute(lo, SLAB, up)
    hi = lax.ppermute(hi, SLAB, down)
    earlier, start = held(earlier, start)
    s_lo = lax.ppermute(start, SLAB, up)
    s_hi = lax.ppermute(start, SLAB, down)
    own = own.reshape(coefficients.shape)
    wide = unpacked(lo, hi).reshape(coefficients.shape)
    v, one, two = begun(start, s_lo, s_hi)
    vectors, rows, early = [start], [], []
    thirds = earlier.shape[1] // 3
    for step in range(depth):
        from_one = lax.ppermute(one, "sub", pairs)
        from_two = lax.ppermute(two, "sub", between)
        rows.append(dots(earlier, vectors))
        more = (s_lo, s_hi) if step == 0 else ()
        after = [rows[-1]]
        if 1 <= step <= 3:
            tied, v = lax.optimization_barrier((earlier, v))
            some = tied[:, (step - 1) * thirds : step * thirds].reshape(tied.shape[0], -1)
            early.append(lax.optimization_barrier(jnp.dot(some, some.T, precision=EXACT)))
            after.append(early[-1])
        out = stepped(step, depth, shifts, own, wide, v, from_one, from_two, more, after)
        if step < depth - 1:
            v, one, two = out
            vectors.append(v[0])
        else:
            vectors.append(out[0])
    rows.append(dots(earlier, vectors))
    block = len(vectors)
    count = start.size * lax.axis_size(SLAB) * lax.axis_size("sub")
    rows, early = lax.optimization_barrier((rows, early))
    rows = jnp.concatenate(rows, axis=0)
    n = earlier.shape[0]
    cross, square, early = packed_total((rows[:, :n], rows[:, n : n + block], sum(early)))
    turned = cross / count
    i = jnp.arange(block)
    own_sum = jnp.where(i[:, None] >= i[None], square, square.T) / count
    new, projection, triangle = finished(
        turned.T, turned, own_sum, early / count, vectors, earlier
    )
    return (jnp.transpose(new, (0, 1, 3, 2, 4)), projection.T, triangle)


def solution(mesh):
    torus = Mesh(
        mesh.devices.reshape(4, 16, 2, mesh.shape["sub"]), ("slab_0", "slab_1", "slab_2", "sub")
    )
    return jax.shard_map(
        body,
        mesh=torus,
        in_specs=(
            P(None, None, None, SLAB, "sub", None),
            P(None, None, SLAB, "sub", None),
            P(None, SLAB, "sub", None),
            P(),
        ),
        out_specs=(P(None, None, SLAB, "sub", None), P(), P()),
        check_vma=False,
    )
```

time: 148 us -> 115 us (0.78)
  blocking collectives: 10.9 us -> 48.6 us
  starting transfers between devices: 79.5 us -> 42.8 us
  local copies, waits for them, and re-layouts: 20.6 us -> 2.15 us
  Pallas kernels: 0 us -> 14.4 us
  matrix products: 13.4 us -> 2.6 us
  waiting for transfers between devices: 12.7 us -> 2.33 us
  other arithmetic: 4.78 us -> 0.28 us
  between operations: 4.61 us -> 0.95 us
    all_to_all x1 -> x2, blocking collectives: 10.9 us -> 48.6 us  [over_copies(): lax.all_to_all(copies, axis, split_axis=0, concat_axis=0, tiled=True)]
    all_to_all x1 -> x0, starting transfers between devices: 20.9 us -> none  [copy_for_each(): return lax.all_to_all(copies, axis, split_axis=0, concat_axis=0, tiled=True)]
    ppermute x20 -> x14, starting transfers between devices: 58.6 us -> 42.8 us  [the longest x5 23.8 us: body(): from_one = lax.ppermute(one, 'sub', pairs)]
    pallas_call x0 -> x16, Pallas kernels: none -> 14.4 us  [the longest x5 5.83 us: stepped(): pl.pallas_call(lambda *refs: step_kernel(step, step == 0, last, *refs[:6...]
    all_to_all x1 -> x0, waiting for transfers between devices: 11.3 us -> none  [copy_for_each(): return lax.all_to_all(copies, axis, split_axis=0, concat_axis=0, tiled=True)]
    dot_general x7 -> x3, matrix products: 12.6 us -> 2.6 us  [body(): jnp.dot(some, some.T, precision=EXACT)]
    another operation x14 -> x0, local copies, waits for them, and re-layouts: 6.2 us -> none  [body(): basis = jnp.stack(vectors)]
    unnamed x17 -> x4, local copies, waits for them, and re-layouts: 4.74 us -> 0.88 us
  transfers between devices with their start and end apart: 21 -> 14, of which waited for: 3 -> 4; matrix products, arithmetic and copies ran while one was open for 14% -> 2% of each run, Pallas kernels for 0% -> 3%
where the time goes in v1:
time: 115 us; the launch traced here: 114 us
  blocking collectives  48.6 us (42%)
  starting transfers between devices  42.8 us (37%)
  Pallas kernels  14.4 us (13%)
  matrix products  2.6 us (2%)
  waiting for transfers between devices  2.33 us (2%)
  local copies, waits for them, and re-layouts  2.15 us (2%)
    all_to_all x2, blocking collectives, over_copies(): lax.all_to_all(copies, axis, split_axis=0, concat_axis=0, tiled=True)  48.6 us
    ppermute x5, starting transfers between devices, body(): from_one = lax.ppermute(one, 'sub', pairs)  23.8 us
    pallas_call x5, Pallas kernels, stepped(): pl.pallas_call(lambda *refs: step_kernel(step, step == 0, last, *refs[:6...  5.83 us
    ppermute x1, starting transfers between devices, body(): hi = lax.ppermute(hi, SLAB, down)  5.19 us
    ppermute x1, starting transfers between devices, body(): lo = lax.ppermute(lo, SLAB, up)  4.94 us
    ppermute x1, starting transfers between devices, body(): s_lo = lax.ppermute(start, SLAB, up)  3.64 us
    ppermute x5, starting transfers between devices, body(): from_two = lax.ppermute(two, 'sub', between)  3.32 us
    pallas_call x1, Pallas kernels, finished(): pl.pallas_call(finish, out_shape=(pltpu.HBM((block, fields, *rest), jnp.f...  2.71 us
  transfers between devices with their start and end apart: 14, of which 4 were waited for; matrix products, arithmetic and copies ran while one was open for 2% of the time, Pallas kernels for 3%

profile of v1, /device:TPU:1, one launch (start us, length us, event | category | flops | bytes accessed | tf_op | source)
XLA Modules:
  0.0 114.2 jit_solution(4244407123855874655)
XLA Ops:
  0.6 0.9 copy-done
  1.5 1.7 %shard_map.67 = (bf16[378,2,8,128]{3,2,1,0:T(8,128)(2,1)S(1)}, bf16[378,8,128]{2,1,0:T(8,128)(2,1)S(1)}, bf16[378,8,128]{2,1,0:T(8,128)(2,1)S(1)}, f32[6,3,8,128]{3,2,1,0:T(8,128)S(1)}) custom-call(bf16[378,2,8,128]{3,2,1,0:T(8,128)(2,1)} %bitcast.48, f32[6,3,8,128]{3,2,1,0:T(8,128)S(1)} %bitcast.45), custom_call_target="tpu_custom_call" | custom-call | flops 1000000 | bytes 4000000 | tf_op jit(solution)/shard_map/pallas_call | solution.py:101
  3.2 4.9 %collective-permute-start = (bf16[378,8,128]{2,1,0:T(8,128)(2,1)S(1)}, bf16[378,8,128]{2,1,0:T(8,128)(2,1)S(1)}, u32[]{:S(2)}, u32[]{:S(2)}) collective-permute-start(bf16[378,8,128]{2,1,0:T(8,128)(2,1)S(1)} %get-tuple-element.46), channel_id=1, source_target_pairs={{0,4},{4,8},{8,12},{12,16},{16,20},{20,24},{24,28},{28,32},{32,36}... | collective-permute-start | bytes 2322440 | tf_op jit(solution)/shard_map/ppermute | solution.py:366
  8.1 5.2 %collective-permute-start.1 = (bf16[378,8,128]{2,1,0:T(8,128)(2,1)S(1)}, bf16[378,8,128]{2,1,0:T(8,128)(2,1)S(1)}, u32[]{:S(2)}, u32[]{:S(2)}) collective-permute-start(bf16[378,8,128]{2,1,0:T(8,128)(2,1)S(1)} %get-tuple-element.47), channel_id=1, source_target_pairs={{4,0},{8,4},{12,8},{16,12},{20,16},{24,20},{28,24},{32,28},{36,32}... | collective-permute-start | bytes 2322440 | tf_op jit(solution)/shard_map/ppermute | solution.py:367
  13.3 1.6 %shard_map.68 = (f32[30,6,3,8,128]{4,3,2,1,0:T(8,128)S(1)}, f32[6,3,8,128]{3,2,1,0:T(8,128)S(1)}) custom-call(f32[30,6,3,8,128]{4,3,2,1,0:T(8,128)} %bitcast.47, f32[6,3,8,128]{3,2,1,0:T(8,128)S(1)} %get-tuple-element.42.s_ref), custom_call_target="tpu_custom_call" | custom-call | flops 100000 | bytes 5000000 | tf_op jit(solution)/shard_map/pallas_call | solution.py:159
  15.0 1.9 %collective-permute-start.3 = (f32[6,3,8,128]{3,2,1,0:T(8,128)S(1)}, f32[6,3,8,128]{3,2,1,0:T(8,128)S(1)}, u32[]{:S(2)}, u32[]{:S(2)}) collective-permute-start(f32[6,3,8,128]{3,2,1,0:T(8,128)S(1)} %get-tuple-element.44.refs_0_.s_ref), channel_id=1, source_target_pairs={{4,0},{8,4},{12,8},{16,12},{20,16},{24,20},{28,24},{32,28},{36,32}... | collective-permute-start | bytes 221192 | tf_op jit(solution)/shard_map/ppermute | solution.py:370
  16.9 3.6 %collective-permute-start.2 = (f32[6,3,8,128]{3,2,1,0:T(8,128)S(1)}, f32[6,3,8,128]{3,2,1,0:T(8,128)S(1)}, u32[]{:S(2)}, u32[]{:S(2)}) collective-permute-start(f32[6,3,8,128]{3,2,1,0:T(8,128)S(1)} %get-tuple-element.44.refs_0_.s_ref), channel_id=1, source_target_pairs={{0,4},{4,8},{8,12},{12,16},{16,20},{20,24},{24,28},{28,32},{32,36}... | collective-permute-start | bytes 221192 | tf_op jit(solution)/shard_map/ppermute | solution.py:369
  20.5 1.5 %collective-permute-done.3.hi_ref.refs_7_ = f32[6,3,8,128]{3,2,1,0:T(8,128)S(1)} collective-permute-done((f32[6,3,8,128]{3,2,1,0:T(8,128)S(1)}, f32[6,3,8,128]{3,2,1,0:T(8,128)S(1)}, u32[]{:S(2)}, u32[]{:S(2)}) %collective-permute-start.3) | collective-permute-done | bytes 73760 | tf_op jit(solution)/shard_map/ppermute | solution.py:370
  22.1 3.1 %collective-permute-start.4 = (f32[2,6,8,128]{3,2,1,0:T(8,128)S(1)}, f32[2,6,8,128]{3,2,1,0:T(8,128)S(1)}, u32[]{:S(2)}, u32[]{:S(2)}) collective-permute-start(f32[2,6,8,128]{3,2,1,0:T(8,128)S(1)} %get-tuple-element.49), channel_id=1, source_target_pairs={{0,1},{1,0},{2,3},{3,2},{4,5},{5,4},{6,7},{7,6},{8,9},{9,8},{10,11... | collective-permute-start | bytes 147464 | tf_op jit(solution)/shard_map/ppermute | solution.py:377
  25.2 0.7 collective-permute-start.5
  25.9 0.3 shard_map.69.refs_8_
  26.3 0.6 shard_map.70
  26.8 0.1 collective-permute-done.4.refs_4_
  27.0 1.3 %shard_map.72 = (f32[2,6,3,8,128]{4,3,2,1,0:T(8,128)S(1)}, f32[2,6,8,128]{3,2,1,0:T(8,128)S(1)}, f32[2,6,8,128]{3,2,1,0:T(8,128)S(1)}) custom-call(f32[5]{0:T(128)S(1)} %copy-done.1, bf16[7,6,6,3,8,128]{5,4,3,2,1,0:T(8,128)(2,1)S(1)} %bitcast.40, bf16[7,6,6,3,8,128]{5,4,3,2,1,0:T(8,128)(2,1)S(1)} %bitcast.35, ...), custom_call_target="tpu_custom_call" | custom-call | flops 10000000 | bytes 3000000 | tf_op jit(solution)/shard_map/pallas_call | solution.py:235
  28.2 6.0 %collective-permute-start.6 = (f32[2,6,8,128]{3,2,1,0:T(8,128)S(1)}, f32[2,6,8,128]{3,2,1,0:T(8,128)S(1)}, u32[]{:S(2)}, u32[]{:S(2)}) collective-permute-start(f32[2,6,8,128]{3,2,1,0:T(8,128)S(1)} %get-tuple-element.53), channel_id=1, source_target_pairs={{0,1},{1,0},{2,3},{3,2},{4,5},{5,4},{6,7},{7,6},{8,9},{9,8},{10,11... | collective-permute-start | bytes 147464 | tf_op jit(solution)/shard_map/ppermute | solution.py:377
  34.3 0.7 collective-permute-start.7
  35.0 0.9 convolution_bitcast_fusion.2.refs_7_
  35.9 0.3 shard_map.73.refs_6_
  36.2 1.2 %shard_map.74 = (f32[2,6,3,8,128]{4,3,2,1,0:T(8,128)S(1)}, f32[2,6,8,128]{3,2,1,0:T(8,128)S(1)}, f32[2,6,8,128]{3,2,1,0:T(8,128)S(1)}) custom-call(f32[5]{0:T(128)S(1)} %copy-done.1, bf16[7,6,6,3,8,128]{5,4,3,2,1,0:T(8,128)(2,1)S(1)} %bitcast.41, bf16[7,6,6,3,8,128]{5,4,3,2,1,0:T(8,128)(2,1)S(1)} %bitcast.36, ...), custom_call_target="tpu_custom_call" | custom-call | flops 10000000 | bytes 3000000 | tf_op jit(solution)/shard_map/pallas_call | solution.py:235
  37.4 4.8 %collective-permute-start.8 = (f32[2,6,8,128]{3,2,1,0:T(8,128)S(1)}, f32[2,6,8,128]{3,2,1,0:T(8,128)S(1)}, u32[]{:S(2)}, u32[]{:S(2)}) collective-permute-start(f32[2,6,8,128]{3,2,1,0:T(8,128)S(1)} %get-tuple-element.58), channel_id=1, source_target_pairs={{0,1},{1,0},{2,3},{3,2},{4,5},{5,4},{6,7},{7,6},{8,9},{9,8},{10,11... | collective-permute-start | bytes 147464 | tf_op jit(solution)/shard_map/ppermute | solution.py:377
  42.2 0.7 collective-permute-start.9
  43.0 0.9 convolution_bitcast_fusion.1.refs_7_
  43.9 0.3 shard_map.75.refs_6_
  44.2 0.2 collective-permute-done.8.refs_4_
  44.4 1.2 %shard_map.76 = (f32[2,6,3,8,128]{4,3,2,1,0:T(8,128)S(1)}, f32[2,6,8,128]{3,2,1,0:T(8,128)S(1)}, f32[2,6,8,128]{3,2,1,0:T(8,128)S(1)}) custom-call(f32[5]{0:T(128)S(1)} %copy-done.1, bf16[7,6,6,3,8,128]{5,4,3,2,1,0:T(8,128)(2,1)S(1)} %bitcast.42, bf16[7,6,6,3,8,128]{5,4,3,2,1,0:T(8,128)(2,1)S(1)} %bitcast.37, ...), custom_call_target="tpu_custom_call" | custom-call | flops 10000000 | bytes 3000000 | tf_op jit(solution)/shard_map/pallas_call | solution.py:235
  45.6 5.1 %collective-permute-start.10 = (f32[2,6,8,128]{3,2,1,0:T(8,128)S(1)}, f32[2,6,8,128]{3,2,1,0:T(8,128)S(1)}, u32[]{:S(2)}, u32[]{:S(2)}) collective-permute-start(f32[2,6,8,128]{3,2,1,0:T(8,128)S(1)} %get-tuple-element.63), channel_id=1, source_target_pairs={{0,1},{1,0},{2,3},{3,2},{4,5},{5,4},{6,7},{7,6},{8,9},{9,8},{10,11... | collective-permute-start | bytes 147464 | tf_op jit(solution)/shard_map/ppermute | solution.py:377
  50.7 0.7 collective-permute-start.11
  51.4 0.9 convolution_bitcast_fusion.refs_7_
  52.3 0.3 shard_map.77.refs_6_
  52.7 1.2 %shard_map.78 = (f32[2,6,3,8,128]{4,3,2,1,0:T(8,128)S(1)}, f32[2,6,8,128]{3,2,1,0:T(8,128)S(1)}, f32[2,6,8,128]{3,2,1,0:T(8,128)S(1)}) custom-call(f32[5]{0:T(128)S(1)} %copy-done.1, bf16[7,6,6,3,8,128]{5,4,3,2,1,0:T(8,128)(2,1)S(1)} %bitcast.43, bf16[7,6,6,3,8,128]{5,4,3,2,1,0:T(8,128)(2,1)S(1)} %bitcast.38, ...), custom_call_target="tpu_custom_call" | custom-call | flops 10000000 | bytes 3000000 | tf_op jit(solution)/shard_map/pallas_call | solution.py:235
  53.9 4.8 %collective-permute-start.12 = (f32[2,6,8,128]{3,2,1,0:T(8,128)S(1)}, f32[2,6,8,128]{3,2,1,0:T(8,128)S(1)}, u32[]{:S(2)}, u32[]{:S(2)}) collective-permute-start(f32[2,6,8,128]{3,2,1,0:T(8,128)S(1)} %get-tuple-element.67), channel_id=1, source_target_pairs={{0,1},{1,0},{2,3},{3,2},{4,5},{5,4},{6,7},{7,6},{8,9},{9,8},{10,11... | collective-permute-start | bytes 147464 | tf_op jit(solution)/shard_map/ppermute | solution.py:377
  58.7 0.7 collective-permute-start.13
  59.4 0.3 shard_map.79.refs_6_
  59.7 0.4 collective-permute-done.12.refs_4_
  60.2 0.9 shard_map.80.refs_5_
  61.1 0.3 shard_map.81
  61.7 0.1 reshape.51
  61.8 0.1 concatenate.7
  61.9 0.1 broadcast_in_dim.4
  62.0 30.1 %all_to_all.10 = f32[32,1,1116]{2,1,0:T(1,128)S(1)} all-to-all(f32[32,1,1116]{2,1,0:T(1,128)S(1)} %broadcast_in_dim.4), channel_id=1, replica_groups=mesh['slab_0'=4,'slab_1'=16,'slab_2'=2,'sub'=4] {'slab_0','slab_2','sub'}, dimensions={0} | all-to-all | bytes 285696 | tf_op jit(solution)/shard_map/all_to_all | solution.py:22
  92.0 0.1 reduce_sum.20
  92.2 18.5 %all_to_all.11 = f32[16,1,1116]{2,1,0:T(1,128)S(1)} all-to-all(f32[16,1,1116]{2,1,0:T(1,128)S(1)} %broadcast_in_dim.10), channel_id=1, replica_groups=mesh['slab_0'=4,'slab_1'=16,'slab_2'=2,'sub'=4] {'slab_1'}, dimensions={0} | all-to-all | bytes 142848 | tf_op jit(solution)/shard_map/all_to_all | solution.py:22
  110.8 0.1 slice_reduce_fusion
  110.9 0.1 fusion.3
  111.2 0.1 copy.31
  111.3 0.1 div.29.early_ref
  111.4 0.1 copy.32.cross_ref
  111.5 2.7 %shard_map.82 = (f32[6,6,3,8,128]{4,3,2,1,0:T(8,128)}, f32[6,30]{1,0:T(8,128)}, f32[6,6]{1,0:T(8,128)}) custom-call(f32[30,6]{1,0:T(8,128)S(1)} %copy.32.cross_ref, f32[6,30]{1,0:T(8,128)S(1)} %div.24.turned_ref, f32[6,6]{1,0:T(8,128)S(1)} %fusion.4.self_ref, f32[30,30]{1,0:T(8,128)S(1)} %div.29.early_ref, ...), custom_call_target="tpu_custom_call" | custom-call | flops 10000000 | bytes 3000000 | tf_op jit(solution)/shard_map/pallas_call | solution.py:336
  (33 shorter events, 0.8 us)
Async XLA Ops:
  0.6 0.9 copy-start
  3.2 23.1 %collective-permute-start = (bf16[378,8,128]{2,1,0:T(8,128)(2,1)S(1)}, bf16[378,8,128]{2,1,0:T(8,128)(2,1)S(1)}, u32[]{:S(2)}, u32[]{:S(2)}) collective-permute-start(bf16[378,8,128]{2,1,0:T(8,128)(2,1)S(1)} %get-tuple-element.46), channel_id=1, source_target_pairs={{0,4},{4,8},{8,12},{12,16},{16,20},{20,24},{24,28},{28,32},{32,36}... | collective-permute-start | bytes 2322440 | tf_op jit(solution)/shard_map/ppermute | solution.py:366
  8.1 18.1 %collective-permute-start.1 = (bf16[378,8,128]{2,1,0:T(8,128)(2,1)S(1)}, bf16[378,8,128]{2,1,0:T(8,128)(2,1)S(1)}, u32[]{:S(2)}, u32[]{:S(2)}) collective-permute-start(bf16[378,8,128]{2,1,0:T(8,128)(2,1)S(1)} %get-tuple-element.47), channel_id=1, source_target_pairs={{4,0},{8,4},{12,8},{16,12},{20,16},{24,20},{28,24},{32,28},{36,32}... | collective-permute-start | bytes 2322440 | tf_op jit(solution)/shard_map/ppermute | solution.py:367
  15.0 7.1 %collective-permute-start.3 = (f32[6,3,8,128]{3,2,1,0:T(8,128)S(1)}, f32[6,3,8,128]{3,2,1,0:T(8,128)S(1)}, u32[]{:S(2)}, u32[]{:S(2)}) collective-permute-start(f32[6,3,8,128]{3,2,1,0:T(8,128)S(1)} %get-tuple-element.44.refs_0_.s_ref), channel_id=1, source_target_pairs={{4,0},{8,4},{12,8},{16,12},{20,16},{24,20},{28,24},{32,28},{36,32}... | collective-permute-start | bytes 221192 | tf_op jit(solution)/shard_map/ppermute | solution.py:370
  16.9 5.2 %collective-permute-start.2 = (f32[6,3,8,128]{3,2,1,0:T(8,128)S(1)}, f32[6,3,8,128]{3,2,1,0:T(8,128)S(1)}, u32[]{:S(2)}, u32[]{:S(2)}) collective-permute-start(f32[6,3,8,128]{3,2,1,0:T(8,128)S(1)} %get-tuple-element.44.refs_0_.s_ref), channel_id=1, source_target_pairs={{0,4},{4,8},{8,12},{12,16},{16,20},{20,24},{24,28},{28,32},{32,36}... | collective-permute-start | bytes 221192 | tf_op jit(solution)/shard_map/ppermute | solution.py:369
  22.1 4.8 %collective-permute-start.4 = (f32[2,6,8,128]{3,2,1,0:T(8,128)S(1)}, f32[2,6,8,128]{3,2,1,0:T(8,128)S(1)}, u32[]{:S(2)}, u32[]{:S(2)}) collective-permute-start(f32[2,6,8,128]{3,2,1,0:T(8,128)S(1)} %get-tuple-element.49), channel_id=1, source_target_pairs={{0,1},{1,0},{2,3},{3,2},{4,5},{5,4},{6,7},{7,6},{8,9},{9,8},{10,11... | collective-permute-start | bytes 147464 | tf_op jit(solution)/shard_map/ppermute | solution.py:377
  25.2 1.7 %collective-permute-start.5 = (f32[2,6,8,128]{3,2,1,0:T(8,128)S(1)}, f32[2,6,8,128]{3,2,1,0:T(8,128)S(1)}, u32[]{:S(2)}, u32[]{:S(2)}) collective-permute-start(f32[2,6,8,128]{3,2,1,0:T(8,128)S(1)} %get-tuple-element.50), channel_id=1, source_target_pairs={{1,2},{2,1},{5,6},{6,5},{9,10},{10,9},{13,14},{14,13},{17,18},{18,... | collective-permute-start | bytes 147464 | tf_op jit(solution)/shard_map/ppermute | solution.py:378
  26.2 0.7 copy-start.1
  28.2 7.9 %collective-permute-start.6 = (f32[2,6,8,128]{3,2,1,0:T(8,128)S(1)}, f32[2,6,8,128]{3,2,1,0:T(8,128)S(1)}, u32[]{:S(2)}, u32[]{:S(2)}) collective-permute-start(f32[2,6,8,128]{3,2,1,0:T(8,128)S(1)} %get-tuple-element.53), channel_id=1, source_target_pairs={{0,1},{1,0},{2,3},{3,2},{4,5},{5,4},{6,7},{7,6},{8,9},{9,8},{10,11... | collective-permute-start | bytes 147464 | tf_op jit(solution)/shard_map/ppermute | solution.py:377
  34.3 1.9 %collective-permute-start.7 = (f32[2,6,8,128]{3,2,1,0:T(8,128)S(1)}, f32[2,6,8,128]{3,2,1,0:T(8,128)S(1)}, u32[]{:S(2)}, u32[]{:S(2)}) collective-permute-start(f32[2,6,8,128]{3,2,1,0:T(8,128)S(1)} %get-tuple-element.54), channel_id=1, source_target_pairs={{1,2},{2,1},{5,6},{6,5},{9,10},{10,9},{13,14},{14,13},{17,18},{18,... | collective-permute-start | bytes 147464 | tf_op jit(solution)/shard_map/ppermute | solution.py:378
  37.4 6.9 %collective-permute-start.8 = (f32[2,6,8,128]{3,2,1,0:T(8,128)S(1)}, f32[2,6,8,128]{3,2,1,0:T(8,128)S(1)}, u32[]{:S(2)}, u32[]{:S(2)}) collective-permute-start(f32[2,6,8,128]{3,2,1,0:T(8,128)S(1)} %get-tuple-element.58), channel_id=1, source_target_pairs={{0,1},{1,0},{2,3},{3,2},{4,5},{5,4},{6,7},{7,6},{8,9},{9,8},{10,11... | collective-permute-start | bytes 147464 | tf_op jit(solution)/shard_map/ppermute | solution.py:377
  42.2 2.1 %collective-permute-start.9 = (f32[2,6,8,128]{3,2,1,0:T(8,128)S(1)}, f32[2,6,8,128]{3,2,1,0:T(8,128)S(1)}, u32[]{:S(2)}, u32[]{:S(2)}) collective-permute-start(f32[2,6,8,128]{3,2,1,0:T(8,128)S(1)} %get-tuple-element.59), channel_id=1, source_target_pairs={{1,2},{2,1},{5,6},{6,5},{9,10},{10,9},{13,14},{14,13},{17,18},{18,... | collective-permute-start | bytes 147464 | tf_op jit(solution)/shard_map/ppermute | solution.py:378
  45.6 7.0 %collective-permute-start.10 = (f32[2,6,8,128]{3,2,1,0:T(8,128)S(1)}, f32[2,6,8,128]{3,2,1,0:T(8,128)S(1)}, u32[]{:S(2)}, u32[]{:S(2)}) collective-permute-start(f32[2,6,8,128]{3,2,1,0:T(8,128)S(1)} %get-tuple-element.63), channel_id=1, source_target_pairs={{0,1},{1,0},{2,3},{3,2},{4,5},{5,4},{6,7},{7,6},{8,9},{9,8},{10,11... | collective-permute-start | bytes 147464 | tf_op jit(solution)/shard_map/ppermute | solution.py:377
  50.7 1.9 %collective-permute-start.11 = (f32[2,6,8,128]{3,2,1,0:T(8,128)S(1)}, f32[2,6,8,128]{3,2,1,0:T(8,128)S(1)}, u32[]{:S(2)}, u32[]{:S(2)}) collective-permute-start(f32[2,6,8,128]{3,2,1,0:T(8,128)S(1)} %get-tuple-element.64), channel_id=1, source_target_pairs={{1,2},{2,1},{5,6},{6,5},{9,10},{10,9},{13,14},{14,13},{17,18},{18,... | collective-permute-start | bytes 147464 | tf_op jit(solution)/shard_map/ppermute | solution.py:378
  53.9 6.3 %collective-permute-start.12 = (f32[2,6,8,128]{3,2,1,0:T(8,128)S(1)}, f32[2,6,8,128]{3,2,1,0:T(8,128)S(1)}, u32[]{:S(2)}, u32[]{:S(2)}) collective-permute-start(f32[2,6,8,128]{3,2,1,0:T(8,128)S(1)} %get-tuple-element.67), channel_id=1, source_target_pairs={{0,1},{1,0},{2,3},{3,2},{4,5},{5,4},{6,7},{7,6},{8,9},{9,8},{10,11... | collective-permute-start | bytes 147464 | tf_op jit(solution)/shard_map/ppermute | solution.py:377
  58.7 1.5 %collective-permute-start.13 = (f32[2,6,8,128]{3,2,1,0:T(8,128)S(1)}, f32[2,6,8,128]{3,2,1,0:T(8,128)S(1)}, u32[]{:S(2)}, u32[]{:S(2)}) collective-permute-start(f32[2,6,8,128]{3,2,1,0:T(8,128)S(1)} %get-tuple-element.68), channel_id=1, source_target_pairs={{1,2},{2,1},{5,6},{6,5},{9,10},{10,9},{13,14},{14,13},{17,18},{18,... | collective-permute-start | bytes 147464 | tf_op jit(solution)/shard_map/ppermute | solution.py:378

commit v2 on v1

--- a/solution.py
+++ b/solution.py
@@ -17,19 +17,13 @@
     return up, [(b, a) for a, b in up]
 
 
+def all_copies(x, axis):
+    copies = jnp.broadcast_to(x, (lax.axis_size(axis), *x.shape))
+    return lax.all_to_all(copies, axis, split_axis=0, concat_axis=0, tiled=True)
+
+
 def over_copies(x, axis):
-    copies = jnp.broadcast_to(x, (lax.axis_size(axis), *x.shape))
-    everything = lax.all_to_all(copies, axis, split_axis=0, concat_axis=0, tiled=True)
-    return jnp.sum(everything, axis=0)
-
-
-def packed_total(arrays):
-    ravelled, at, done = (jnp.concatenate([a.reshape(-1) for a in arrays]), 0, [])
-    so_far = over_copies(over_copies(ravelled[None], NEAR), FAR)[0]
-    for a in arrays:
-        done.append(so_far[at : at + a.size].reshape(a.shape))
-        at += a.size
-    return tuple(done)
+    return jnp.sum(all_copies(x, axis), axis=0)
 
 
 def swap_halves(x):
@@ -40,22 +34,25 @@
     return lax.broadcasted_iota(jnp.int32, shape, len(shape) - 2) < shape[-2] // 2
 
 
-def pack(c_ref, s_ref, own_ref, lo_ref, hi_ref, start_ref, sems):
-    parts = sems.shape[0]
+def pack(c_ref, s_ref, own_ref, lo_ref, hi_ref, start_ref, one_ref, two_ref, raw, sems):
+    parts = sems.shape[0] - 1
+    begin = pltpu.make_async_copy(s_ref, start_ref, sems.at[parts])
+    begin.start()
     size = c_ref.shape[0] // parts
     copies = [
         pltpu.make_async_copy(
-            c_ref.at[pl.ds(n * size, size)], own_ref.at[pl.ds(n * size, size)], sems.at[n]
+            c_ref.at[pl.ds(n * size, size)], raw.at[pl.ds(n * size, size)], sems.at[n]
         )
         for n in range(parts)
     ]
     for copy in copies:
         copy.start()
-    start_ref[...] = s_ref[...]
     first = half_mask(c_ref.shape[2:])
 
     def pair(p, carry):
-        a, b = own_ref[p, 0].astype(jnp.float32), own_ref[p, 1].astype(jnp.float32)
+        a, b = raw[p, 0].astype(jnp.float32), raw[p, 1].astype(jnp.float32)
+        own_ref[p, 0] = a
+        own_ref[p, 1] = b
         hi_ref[p] = jnp.where(first, a, swap_halves(b)).astype(hi_ref.dtype)
         lo_ref[p] = jnp.where(first, swap_halves(a), b).astype(lo_ref.dtype)
         return carry
@@ -63,6 +60,11 @@
     for n, copy in enumerate(copies):
         copy.wait()
         lax.fori_loop(n * size, (n + 1) * size, pair, 0, unroll=9)
+    begin.wait()
+    odd = is_odd()
+    near, far = start_ref[:, 0], start_ref[:, start_ref.shape[1] - 1]
+    one_ref[...] = jnp.where(odd, near, far)
+    two_ref[...] = jnp.where(odd, far, near)
 
 
 def unpack(lo_ref, hi_ref, wide_ref):
@@ -70,8 +72,8 @@
 
     def pair(p, carry):
         lo, hi = lo_ref[p].astype(jnp.float32), hi_ref[p].astype(jnp.float32)
-        wide_ref[p, 0] = jnp.where(first, hi, swap_halves(lo)).astype(wide_ref.dtype)
-        wide_ref[p, 1] = jnp.where(first, swap_halves(hi), lo).astype(wide_ref.dtype)
+        wide_ref[p, 0] = jnp.where(first, hi, swap_halves(lo))
+        wide_ref[p, 1] = jnp.where(first, swap_halves(hi), lo)
         return carry
 
     lax.fori_loop(0, lo_ref.shape[0], pair, 0, unroll=9)
@@ -98,23 +100,29 @@
 def packed(coefficients, start):
     pairs = coefficients.reshape(-1, 2, *coefficients.shape[-2:])
     half = pltpu.VMEM((pairs.shape[0], *pairs.shape[2:]), pairs.dtype)
+    edge = pltpu.VMEM((start.shape[0], *start.shape[2:]), start.dtype)
     return pl.pallas_call(
         pack,
         out_shape=(
-            pltpu.VMEM(pairs.shape, pairs.dtype), half, half, pltpu.VMEM(start.shape, start.dtype)
+            pltpu.VMEM(pairs.shape, jnp.float32),
+            half,
+            half,
+            pltpu.VMEM(start.shape, start.dtype),
+            edge,
+            edge,
         ),
-        in_specs=[pl.BlockSpec(memory_space=pltpu.HBM), VMEM],
-        out_specs=(VMEM,) * 4,
-        scratch_shapes=[pltpu.SemaphoreType.DMA((6,))],
+        in_specs=[pl.BlockSpec(memory_space=pltpu.HBM)] * 2,
+        out_specs=(VMEM,) * 6,
+        scratch_shapes=[pltpu.VMEM(pairs.shape, pairs.dtype), pltpu.SemaphoreType.DMA((7,))],
         compiler_params=LIMIT,
         cost_estimate=cost(10**6, 4 * 10**6),
-    )(in_hbm(pairs), in_vmem(start))
+    )(in_hbm(pairs), in_hbm(start))
 
 
 def unpacked(lo, hi):
     return pl.pallas_call(
         unpack,
-        out_shape=pltpu.VMEM((lo.shape[0], 2, *lo.shape[1:]), lo.dtype),
+        out_shape=pltpu.VMEM((lo.shape[0], 2, *lo.shape[1:]), jnp.float32),
         in_specs=[VMEM] * 2,
         out_specs=VMEM,
         compiler_params=LIMIT,
@@ -126,45 +134,62 @@
     return lax.rem(lax.axis_index("sub"), 2) > 0
 
 
-def begin_kernel(s_ref, lo_ref, hi_ref, v_ref, one_ref, two_ref):
+def both_kernel(s_ref, one_ref, two_ref, up_ref, down_ref):
+    odd = is_odd()
     columns = s_ref.shape[1]
-    v_ref[0] = s_ref[...]
-    v_ref[1] = jnp.where(half_mask(s_ref.shape), hi_ref[...], lo_ref[...])
+    low = half_mask(s_ref.shape[2:])
+    for e in range(s_ref.shape[0]):
+        one, two = one_ref[e], two_ref[e]
+        left, right = jnp.where(odd, one, two), jnp.where(odd, two, one)
+        up_ref[e, :columns] = s_ref[e]
+        down_ref[e, :columns] = s_ref[e]
+        up_ref[e, columns] = jnp.where(low, swap_halves(left), right)
+        down_ref[e, columns] = jnp.where(low, left, swap_halves(right))
+
+
+def begin_kernel(s_ref, lo_ref, hi_ref, one_ref, two_ref, v_ref, first_ref, second_ref):
     odd = is_odd()
-    near, far = v_ref[:, :, 0], v_ref[:, :, columns - 1]
-    one_ref[...] = jnp.where(odd, near, far)
-    two_ref[...] = jnp.where(odd, far, near)
-
-
-def begun(start, s_lo, s_hi):
-    edge = pltpu.VMEM((2, start.shape[0], *start.shape[2:]), start.dtype)
-    return pl.pallas_call(
-        begin_kernel,
-        out_shape=(pltpu.VMEM((2, *start.shape), start.dtype), edge, edge),
-        in_specs=[VMEM] * 3,
-        out_specs=(VMEM,) * 3,
+    columns = s_ref.shape[1]
+    low = half_mask(s_ref.shape[2:])
+    for e in range(s_ref.shape[0]):
+        for x in range(columns):
+            v_ref[0, e, x] = s_ref[e, x]
+            v_ref[1, e, x] = jnp.where(low, hi_ref[e, x], lo_ref[e, x])
+        lo, hi = lo_ref[e, columns], hi_ref[e, columns]
+        left = jnp.where(low, hi, swap_halves(lo))
+        right = jnp.where(low, swap_halves(hi), lo)
+        first_ref[0, e], second_ref[0, e] = one_ref[e], two_ref[e]
+        first_ref[1, e] = jnp.where(odd, left, right)
+        second_ref[1, e] = jnp.where(odd, right, left)
+
+
+def small_call(kernel, outs, *operands):
+    return pl.pallas_call(
+        kernel,
+        out_shape=tuple(pltpu.VMEM(shape, jnp.float32) for shape in outs),
+        in_specs=[VMEM] * len(operands),
+        out_specs=(VMEM,) * len(outs),
         compiler_params=LIMIT,
         cost_estimate=cost(10**5, 10**5),
-    )(*(in_vmem(x) for x in (start, s_lo, s_hi)))
-
-
-def early_kernel(e_ref, s_ref, held_ref, start_ref, sem):
+    )(*(in_vmem(x) for x in operands))
+
+
+def early_kernel(e_ref, after_ref, held_ref, sem):
     copy = pltpu.make_async_copy(e_ref, held_ref, sem.at[0])
     copy.start()
-    start_ref[...] = s_ref[...]
     copy.wait()
 
 
-def held(earlier, start):
+def held(earlier, after):
     return pl.pallas_call(
         early_kernel,
-        out_shape=(pltpu.VMEM(earlier.shape, earlier.dtype), pltpu.VMEM(start.shape, start.dtype)),
-        in_specs=[pl.BlockSpec(memory_space=pltpu.HBM), VMEM],
-        out_specs=(VMEM,) * 2,
+        out_shape=pltpu.VMEM(earlier.shape, earlier.dtype),
+        in_specs=[pl.BlockSpec(memory_space=pltpu.HBM), ANY],
+        out_specs=VMEM,
         scratch_shapes=[pltpu.SemaphoreType.DMA((1,))],
         compiler_params=LIMIT,
         cost_estimate=cost(10**5, 5 * 10**6),
-    )(in_hbm(earlier), in_vmem(start))
+    )(in_hbm(earlier), after)
 
 
 def step_kernel(step, first_step, last_step, shifts_ref, *refs):
@@ -210,7 +235,7 @@
                 for c in range(comps):
                     total = acc[t][c]
                     for d, f in enumerate(fields):
-                        term = source[d, c, e, x].astype(jnp.float32) * f
+                        term = source[d, c, e, x] * f
                         total = term if total is None else total + term
                     acc[t][c] = total
         for t in range(len(acc)):
@@ -244,8 +269,12 @@
     )(shifts, *(in_vmem(a) for a in (own, wide, v, one, two, *more)), *after)
 
 
-def dots_kernel(e_ref, *refs):
-    *w_refs, out_ref, part = refs
+LANES = 128
+SLOT = 32
+STRIDE = 40
+
+
+def dots_row(e_ref, w_refs, part):
     count, comps, columns = e_ref.shape[:3]
     v_ref = w_refs[-1]
     part[...] = jnp.zeros_like(part)
@@ -263,43 +292,131 @@
         for n, total in enumerate(acc):
             part[at + n : at + n + 1] = jnp.sum(total, axis=0, keepdims=True)
     ones = jnp.ones((8, part.shape[1]), jnp.float32)
-    out_ref[...] = lax.dot_general(
+    return lax.dot_general(
         ones, part[...], (((1,), (1,)), ((), ())), precision=EXACT,
         preferred_element_type=jnp.float32,
     )[:1]
 
 
+def dots_kernel(e_ref, *refs):
+    *w_refs, out_ref, part = refs
+    out_ref[...] = dots_row(e_ref, w_refs, part)
+
+
 def dots(earlier, vectors):
-    width = 40
     return pl.pallas_call(
         dots_kernel,
-        out_shape=pltpu.VMEM((1, width), jnp.float32),
+        out_shape=pltpu.VMEM((1, LANES), jnp.float32),
         in_specs=[VMEM] * (1 + len(vectors)),
         out_specs=VMEM,
-        scratch_shapes=[pltpu.VMEM((width, vectors[0].shape[-1]), jnp.float32)],
+        scratch_shapes=[pltpu.VMEM((LANES, LANES), jnp.float32)],
         compiler_params=LIMIT,
         cost_estimate=cost(10**6, 3 * 10**6),
     )(in_vmem(earlier), *(in_vmem(v) for v in vectors))
 
 
-def finish(cross_ref, turned_ref, self_ref, early_ref, e_ref, *refs):
-    block = self_ref.shape[0]
-    w_refs, (out_ref, proj_ref, tri_ref, o_vmem, small, spread, sems) = refs[:block], refs[block:]
-    count = cross_ref.shape[0]
-    p = cross_ref[...]
-    proj = pltpu.make_async_copy(turned_ref, proj_ref, sems.at[0])
+def lane_roll(x, shift):
+    shift %= LANES
+    return pltpu.roll(x, shift, 1) if shift else x
+
+
+def folds(count):
+    for j in range(count // 2):
+        yield j, count - 1 - j, j // (LANES // SLOT), SLOT * (j % (LANES // SLOT))
+
+
+def tiles_of(count, block):
+    early = -(-(count // 2) * SLOT // LANES)
+    per = LANES // STRIDE
+    return early, per, early + -(-block // per)
+
+
+def message_kernel(block, sums, e_ref, *refs):
+    w_refs, refs = refs[:block], refs[block:]
+    rows, refs = refs[: block - 1], refs[block - 1 :]
+    parts, (out_ref, part, square) = refs[:sums], refs[sums:]
+    count = e_ref.shape[0]
+    early, per, total = tiles_of(count, block)
+    square[...] = jnp.zeros_like(square)
+    square[:count, :count] = sum(p[...] for p in parts)
+    lane = lax.broadcasted_iota(jnp.int32, (1, LANES), 1)
+    tiles = [jnp.zeros((1, LANES), jnp.float32) for _ in range(total)]
+    for j, r, q, at in folds(count):
+        upper = lane_roll(square[j : j + 1], at + 1)
+        lower = lane_roll(square[r : r + 1], at - r)
+        tiles[q] = jnp.where(
+            (lane > at + j) & (lane <= at + count),
+            upper,
+            jnp.where((lane >= at) & (lane <= at + j), lower, tiles[q]),
+        )
+    last = dots_row(e_ref, w_refs, part)
+    for k in range(block):
+        row = last if k == block - 1 else rows[k][...]
+        t = early + k // per
+        tiles[t] = tiles[t] + lane_roll(row, STRIDE * (k % per))
+    for t in range(total):
+        out_ref[:, t * LANES : (t + 1) * LANES] = tiles[t]
+
+
+def message(earlier, vectors, rows, parts):
+    count, block = earlier.shape[0], len(vectors)
+    width = LANES * tiles_of(count, block)[2]
+    operands = (earlier, *vectors, *rows, *parts)
+    return pl.pallas_call(
+        lambda *refs: message_kernel(block, len(parts), *refs),
+        out_shape=pltpu.VMEM((1, width), jnp.float32),
+        in_specs=[VMEM] * len(operands),
+        out_specs=VMEM,
+        scratch_shapes=[
+            pltpu.VMEM((LANES, LANES), jnp.float32),
+            pltpu.VMEM((SLOT, LANES), jnp.float32),
+        ],
+        compiler_params=LIMIT,
+        cost_estimate=cost(10**6, 3 * 10**6),
+    )(*(in_vmem(x) for x in operands))
+
+
+def against(a, b):
+    return lax.dot_general(
+        a, b, (((1,), (1,)), ((), ())), precision=EXACT, preferred_element_type=jnp.float32
+    )
+
+
+def finish(block, scale, m_ref, e_ref, *refs):
+    w_refs, refs = refs[:block], refs[block:]
+    out_ref, proj_ref, tri_ref, o_vmem, small, turned_vmem, square, lines, spread, sems = refs
+    count = e_ref.shape[0]
+    early, per, total = tiles_of(count, block)
+    tiles = [
+        jnp.sum(m_ref[:, t * LANES : (t + 1) * LANES], axis=0, keepdims=True) * scale
+        for t in range(total)
+    ]
+    lane = lax.broadcasted_iota(jnp.int32, (1, LANES), 1)
+    for k in range(block):
+        lines[k : k + 1] = lane_roll(tiles[early + k // per], -STRIDE * (k % per))
+    for j, r, q, at in folds(count):
+        upper = jnp.where(lane >= j, lane_roll(tiles[q], -at - 1), 0.0)
+        lower = jnp.where(lane >= r, lane_roll(tiles[q], r - at), 0.0)
+        square[j : j + 1] = jnp.where(lane == j, 0.5 * upper, upper)
+        square[r : r + 1] = jnp.where(lane == r, 0.5 * lower, lower)
+    turned = lines[:block, :count]
+    turned_vmem[...] = turned
+    proj = pltpu.make_async_copy(turned_vmem, proj_ref, sems.at[0])
     proj.start()
-    part = jnp.dot(early_ref[...], p, precision=EXACT) - 2.0 * p
-    gram = self_ref[...] + jnp.dot(turned_ref[...], part, precision=EXACT)
     row = lax.broadcasted_iota(jnp.int32, (block, block), 0)
     col = lax.broadcasted_iota(jnp.int32, (block, block), 1)
     unit = jnp.where(row == col, 1.0, 0.0)
-    a = jnp.concatenate([gram, unit, -turned_ref[...]], axis=1)
+    inner = lines[:block, count : count + block]
+    inner = jnp.where(row > col, inner, jnp.where(row == col, 0.5 * inner, 0.0))
+    part = jnp.dot(turned, square[:count, :count], precision=EXACT) - turned
+    gram = inner + against(part, turned)
+    gram = gram + against(unit, gram)
+    a = jnp.concatenate([gram, unit, -turned], axis=1)
     rows = lax.broadcasted_iota(jnp.int32, a.shape, 0)
     for k in range(block):
-        scale = 1.0 / jnp.sqrt(a[k : k + 1, k : k + 1])
-        pivot = a[k : k + 1] * scale
-        factor = a[:, k : k + 1] * scale
+        inverse = 1.0 / jnp.sqrt(a[k : k + 1, k : k + 1])
+        pivot = a[k : k + 1] * inverse
+        factor = a[:, k : k + 1] * inverse
         a = jnp.where(rows == k, pivot, jnp.where(rows > k, a - factor * pivot, a))
     small[...] = jnp.where(row <= col, a[:, :block], 0.0)
     tri = pltpu.make_async_copy(small, tri_ref, sems.at[1])
@@ -330,27 +447,31 @@
         c.wait()
 
 
-def finished(cross, turned, self_sum, early, vectors, earlier):
-    block = len(vectors)
+def finished(everything, total, vectors, earlier):
+    block, count = len(vectors), earlier.shape[0]
     fields, *rest = vectors[0].shape
-    return pl.pallas_call(
-        finish,
+    operands = (everything, earlier, *vectors)
+    return pl.pallas_call(
+        lambda *refs: finish(block, 1.0 / total, *refs),
         out_shape=(
             pltpu.HBM((block, fields, *rest), jnp.float32),
-            pltpu.HBM(turned.shape, jnp.float32),
-            pltpu.HBM(self_sum.shape, jnp.float32),
+            pltpu.HBM((block, count), jnp.float32),
+            pltpu.HBM((block, block), jnp.float32),
         ),
-        in_specs=[VMEM] * (5 + block),
+        in_specs=[VMEM] * len(operands),
         out_specs=(pl.BlockSpec(memory_space=pltpu.HBM),) * 3,
         scratch_shapes=[
             pltpu.VMEM((fields // 2, block, 2, *rest), jnp.float32),
-            pltpu.VMEM(self_sum.shape, jnp.float32),
-            pltpu.VMEM((block + earlier.shape[0], block, *rest[1:]), jnp.float32),
+            pltpu.VMEM((block, block), jnp.float32),
+            pltpu.VMEM((block, count), jnp.float32),
+            pltpu.VMEM((SLOT, LANES), jnp.float32),
+            pltpu.VMEM((8, LANES), jnp.float32),
+            pltpu.VMEM((block + count, block, *rest[1:]), jnp.float32),
             pltpu.SemaphoreType.DMA((2 + fields // 2,)),
         ],
         compiler_params=LIMIT,
         cost_estimate=cost(10**7, 3 * 10**6),
-    )(*(in_vmem(x) for x in (cross, turned, self_sum, early, earlier, *vectors)))
+    )(*(in_vmem(x) for x in operands))
 
 
 def body(coefficients, earlier, start, shifts):
@@ -362,20 +483,31 @@
     columns = lax.axis_size("sub")
     pairs = [(i, i ^ 1) for i in range(columns)]
     between = [(i, ((i + 1) ^ 1) - 1) for i in range(1, columns - 1)]
-    own, lo, hi, start = packed(coefficients, start)
+    own, lo, hi, start, one, two = packed(coefficients, start)
     lo = lax.ppermute(lo, SLAB, up)
     hi = lax.ppermute(hi, SLAB, down)
-    earlier, start = held(earlier, start)
-    s_lo = lax.ppermute(start, SLAB, up)
-    s_hi = lax.ppermute(start, SLAB, down)
+    fields, width, *plane = start.shape
+    from_one = lax.ppermute(one, "sub", pairs)
+    from_two = lax.ppermute(two, "sub", between)
+    s_lo, s_hi = small_call(
+        both_kernel, [(fields, width + 1, *plane)] * 2, start, from_one, from_two
+    )
+    earlier = held(earlier, s_hi)
+    s_lo = lax.ppermute(s_lo, SLAB, up)
+    s_hi = lax.ppermute(s_hi, SLAB, down)
     own = own.reshape(coefficients.shape)
     wide = unpacked(lo, hi).reshape(coefficients.shape)
-    v, one, two = begun(start, s_lo, s_hi)
+    v, from_one, from_two = small_call(
+        begin_kernel,
+        [(2, *start.shape)] + [(2, fields, *plane)] * 2,
+        start, s_lo, s_hi, from_one, from_two,
+    )
     vectors, rows, early = [start], [], []
     thirds = earlier.shape[1] // 3
     for step in range(depth):
-        from_one = lax.ppermute(one, "sub", pairs)
-        from_two = lax.ppermute(two, "sub", between)
+        if step:
+            from_one = lax.ppermute(one, "sub", pairs)
+            from_two = lax.ppermute(two, "sub", between)
         rows.append(dots(earlier, vectors))
         more = (s_lo, s_hi) if step == 0 else ()
         after = [rows[-1]]
@@ -390,19 +522,10 @@
             vectors.append(v[0])
         else:
             vectors.append(out[0])
-    rows.append(dots(earlier, vectors))
-    block = len(vectors)
-    count = start.size * lax.axis_size(SLAB) * lax.axis_size("sub")
-    rows, early = lax.optimization_barrier((rows, early))
-    rows = jnp.concatenate(rows, axis=0)
-    n = earlier.shape[0]
-    cross, square, early = packed_total((rows[:, :n], rows[:, n : n + block], sum(early)))
-    turned = cross / count
-    i = jnp.arange(block)
-    own_sum = jnp.where(i[:, None] >= i[None], square, square.T) / count
-    new, projection, triangle = finished(
-        turned.T, turned, own_sum, early / count, vectors, earlier
-    )
+    total = start.size * lax.axis_size(SLAB) * lax.axis_size("sub")
+    near = over_copies(message(earlier, vectors, rows, early), NEAR)
+    everything = all_copies(near, FAR)[:, 0]
+    new, projection, triangle = finished(everything, total, vectors, earlier)
     return (jnp.transpose(new, (0, 1, 3, 2, 4)), projection.T, triangle)
 
 

time: 115 us -> 111 us (0.965)
  starting transfers between devices: 42.8 us -> 39.4 us
  waiting for transfers between devices: 2.33 us -> 4.13 us
  local copies, waits for them, and re-layouts: 2.15 us -> 0.41 us
    ppermute x5, starting transfers between devices: 23.8 us -> 21.6 us  [body(): from_one = lax.ppermute(one, 'sub', pairs)]
    ppermute x5, waiting for transfers between devices: 0.76 us -> 2.61 us  [body(): from_one = lax.ppermute(one, 'sub', pairs)]
    ppermute x2, starting transfers between devices: 5.56 us -> 4.33 us  [the longest x1 2.41 us: body(): s_hi = lax.ppermute(s_hi, SLAB, down)]
    pallas_call x10 -> x11, Pallas kernels: 8.04 us -> 8.72 us  [the longest x1 2.93 us: finished(): pl.pallas_call(lambda *refs: finish(block, 1.0 / total, *refs), out_shape...]
  transfers between devices with their start and end apart: 14 -> 14, of which waited for: 4 -> 3; matrix products, arithmetic and copies ran while one was open for 2% -> 3% of each run, Pallas kernels for 3% -> 3%
where the time goes in v2:
time: 111 us; the launch traced here: 110 us
  blocking collectives  48.1 us (43%)
  starting transfers between devices  39.4 us (35%)
  Pallas kernels  14.4 us (13%)
  waiting for transfers between devices  4.13 us (4%)
  matrix products  2.6 us (2%)
    all_to_all x2, blocking collectives, all_copies(): return lax.all_to_all(copies, axis, split_axis=0, concat_axis=0, tiled=True)  48.1 us
    ppermute x5, starting transfers between devices, body(): from_one = lax.ppermute(one, 'sub', pairs)  21.6 us
    pallas_call x5, Pallas kernels, stepped(): pl.pallas_call(lambda *refs: step_kernel(step, step == 0, last, *refs[:6...  5.2 us
    ppermute x1, starting transfers between devices, body(): hi = lax.ppermute(hi, SLAB, down)  5.19 us
    ppermute x1, starting transfers between devices, body(): lo = lax.ppermute(lo, SLAB, up)  4.94 us
    ppermute x5, starting transfers between devices, body(): from_two = lax.ppermute(two, 'sub', between)  3.32 us
    pallas_call x1, Pallas kernels, finished(): pl.pallas_call(lambda *refs: finish(block, 1.0 / total, *refs), out_shape...  2.93 us
    ppermute x5, waiting for transfers between devices, body(): from_one = lax.ppermute(one, 'sub', pairs)  2.61 us
  transfers between devices with their start and end apart: 14, of which 3 were waited for; matrix products, arithmetic and copies ran while one was open for 3% of the time, Pallas kernels for 3%

profile of v2, /device:TPU:1, one launch (start us, length us, event | category | flops | bytes accessed | tf_op | source)
XLA Modules:
  0.0 110.0 jit_solution(4320602385221879724)
XLA Ops:
  0.6 1.7 %shard_map.67 = (f32[378,2,8,128]{3,2,1,0:T(8,128)S(1)}, bf16[378,8,128]{2,1,0:T(8,128)(2,1)S(1)}, bf16[378,8,128]{2,1,0:T(8,128)(2,1)S(1)}, f32[6,3,8,128]{3,2,...) custom-call(bf16[378,2,8,128]{3,2,1,0:T(8,128)(2,1)} %bitcast.44, f32[6,3,8,128]{3,2,1,0:T(8,128)} %bitcast.45), custom_call_target="tpu_custom_call" | custom-call | flops 1000000 | bytes 4000000 | tf_op jit(solution)/shard_map/pallas_call | solution.py:104
  2.3 4.9 %collective-permute-start.2 = (bf16[378,8,128]{2,1,0:T(8,128)(2,1)S(1)}, bf16[378,8,128]{2,1,0:T(8,128)(2,1)S(1)}, u32[]{:S(2)}, u32[]{:S(2)}) collective-permute-start(bf16[378,8,128]{2,1,0:T(8,128)(2,1)S(1)} %get-tuple-element.40), channel_id=1, source_target_pairs={{0,4},{4,8},{8,12},{12,16},{16,20},{20,24},{24,28},{28,32},{32,36}... | collective-permute-start | bytes 2322440 | tf_op jit(solution)/shard_map/ppermute | solution.py:487
  7.3 5.2 %collective-permute-start.3 = (bf16[378,8,128]{2,1,0:T(8,128)(2,1)S(1)}, bf16[378,8,128]{2,1,0:T(8,128)(2,1)S(1)}, u32[]{:S(2)}, u32[]{:S(2)}) collective-permute-start(bf16[378,8,128]{2,1,0:T(8,128)(2,1)S(1)} %get-tuple-element.41), channel_id=1, source_target_pairs={{4,0},{8,4},{12,8},{16,12},{20,16},{24,20},{28,24},{32,28},{36,32}... | collective-permute-start | bytes 2322440 | tf_op jit(solution)/shard_map/ppermute | solution.py:488
  12.5 1.9 %collective-permute-start = (f32[6,8,128]{2,1,0:T(8,128)S(1)}, f32[6,8,128]{2,1,0:T(8,128)S(1)}, u32[]{:S(2)}, u32[]{:S(2)}) collective-permute-start(f32[6,8,128]{2,1,0:T(8,128)S(1)} %get-tuple-element.36), channel_id=1, source_target_pairs={{0,1},{1,0},{2,3},{3,2},{4,5},{5,4},{6,7},{7,6},{8,9},{9,8},{10,11... | collective-permute-start | bytes 73736 | tf_op jit(solution)/shard_map/ppermute | solution.py:490
  14.4 0.7 collective-permute-start.1
  15.1 2.2 %collective-permute-done.one_ref = f32[6,8,128]{2,1,0:T(8,128)S(1)} collective-permute-done((f32[6,8,128]{2,1,0:T(8,128)S(1)}, f32[6,8,128]{2,1,0:T(8,128)S(1)}, u32[]{:S(2)}, u32[]{:S(2)}) %collective-permute-start) | collective-permute-done | bytes 24608 | tf_op jit(solution)/shard_map/ppermute | solution.py:490
  17.3 1.9 %collective-permute-start.4 = (f32[6,4,8,128]{3,2,1,0:T(8,128)S(1)}, f32[6,4,8,128]{3,2,1,0:T(8,128)S(1)}, u32[]{:S(2)}, u32[]{:S(2)}) collective-permute-start(f32[6,4,8,128]{3,2,1,0:T(8,128)S(1)} %get-tuple-element.42), channel_id=1, source_target_pairs={{0,4},{4,8},{8,12},{12,16},{16,20},{20,24},{24,28},{28,32},{32,36}... | collective-permute-start | bytes 294920 | tf_op jit(solution)/shard_map/ppermute | solution.py:496
  19.2 2.4 %collective-permute-start.5 = (f32[6,4,8,128]{3,2,1,0:T(8,128)S(1)}, f32[6,4,8,128]{3,2,1,0:T(8,128)S(1)}, u32[]{:S(2)}, u32[]{:S(2)}) collective-permute-start(f32[6,4,8,128]{3,2,1,0:T(8,128)S(1)} %get-tuple-element.38.after_ref), channel_id=1, source_target_pairs={{4,0},{8,4},{12,8},{16,12},{20,16},{24,20},{28,24},{32,28},{36,32}... | collective-permute-start | bytes 294920 | tf_op jit(solution)/shard_map/ppermute | solution.py:497
  21.7 1.6 %shard_map.69.e_ref.refs_0_.refs_1_ = f32[30,6,3,8,128]{4,3,2,1,0:T(8,128)S(1)} custom-call(f32[30,6,3,8,128]{4,3,2,1,0:T(8,128)} %bitcast.43, f32[6,4,8,128]{3,2,1,0:T(8,128)S(1)} %get-tuple-element.38.after_ref), custom_call_target="tpu_custom_call" | custom-call | flops 100000 | bytes 5000000 | tf_op jit(solution)/shard_map/pallas_call | solution.py:184
  23.3 0.4 shard_map.72.refs_8_.refs_7_
  23.7 1.5 %collective-permute-done.5.hi_ref.refs_7_ = f32[6,4,8,128]{3,2,1,0:T(8,128)S(1)} collective-permute-done((f32[6,4,8,128]{3,2,1,0:T(8,128)S(1)}, f32[6,4,8,128]{3,2,1,0:T(8,128)S(1)}, u32[]{:S(2)}, u32[]{:S(2)}) %collective-permute-start.5) | collective-permute-done | bytes 98336 | tf_op jit(solution)/shard_map/ppermute | solution.py:497
  25.2 0.0 copy-start
  25.2 0.0 collective-permute-done.2.lo_ref
  25.2 0.5 shard_map.70
  25.7 0.1 copy-done
  25.9 1.1 %shard_map.73 = (f32[2,6,3,8,128]{4,3,2,1,0:T(8,128)S(1)}, f32[2,6,8,128]{3,2,1,0:T(8,128)S(1)}, f32[2,6,8,128]{3,2,1,0:T(8,128)S(1)}) custom-call(f32[5]{0:T(128)S(1)} %copy-done, f32[7,6,6,3,8,128]{5,4,3,2,1,0:T(8,128)S(1)} %bitcast.37, f32[7,6,6,3,8,128]{5,4,3,2,1,0:T(8,128)S(1)} %bitcast.32, f32[2,6,3,8,128]{4,3,2,1,0:T(8,128)S(1)} %get-tuple-element.43.refs_3_, ...), custom_call_target="tpu_custom_call" | custom-call | flops 10000000 | bytes 3000000 | tf_op jit(solution)/shard_map/pallas_call | solution.py:260
  27.0 5.5 %collective-permute-start.6 = (f32[2,6,8,128]{3,2,1,0:T(8,128)S(1)}, f32[2,6,8,128]{3,2,1,0:T(8,128)S(1)}, u32[]{:S(2)}, u32[]{:S(2)}) collective-permute-start(f32[2,6,8,128]{3,2,1,0:T(8,128)S(1)} %get-tuple-element.48), channel_id=1, source_target_pairs={{0,1},{1,0},{2,3},{3,2},{4,5},{5,4},{6,7},{7,6},{8,9},{9,8},{10,11... | collective-permute-start | bytes 147464 | tf_op jit(solution)/shard_map/ppermute | solution.py:509
  32.5 0.7 collective-permute-start.7
  33.2 0.9 convolution_bitcast_fusion.2.refs_7_.refs_12_
  34.1 0.4 shard_map.74.refs_6_.refs_8_
  34.4 0.0 collective-permute-done.6.refs_4_
  34.5 0.0 collective-permute-done.7.refs_5_
  34.5 1.1 shard_map.75
  35.6 4.7 %collective-permute-start.8 = (f32[2,6,8,128]{3,2,1,0:T(8,128)S(1)}, f32[2,6,8,128]{3,2,1,0:T(8,128)S(1)}, u32[]{:S(2)}, u32[]{:S(2)}) collective-permute-start(f32[2,6,8,128]{3,2,1,0:T(8,128)S(1)} %get-tuple-element.53), channel_id=1, source_target_pairs={{0,1},{1,0},{2,3},{3,2},{4,5},{5,4},{6,7},{7,6},{8,9},{9,8},{10,11... | collective-permute-start | bytes 147464 | tf_op jit(solution)/shard_map/ppermute | solution.py:509
  40.3 0.7 collective-permute-start.9
  41.0 0.9 convolution_bitcast_fusion.1.refs_7_.refs_13_
  41.9 0.4 shard_map.76.refs_6_.refs_9_
  42.3 0.0 collective-permute-done.8.refs_4_
  42.3 0.0 collective-permute-done.9.refs_5_
  42.3 1.1 shard_map.77
  43.4 4.8 %collective-permute-start.10 = (f32[2,6,8,128]{3,2,1,0:T(8,128)S(1)}, f32[2,6,8,128]{3,2,1,0:T(8,128)S(1)}, u32[]{:S(2)}, u32[]{:S(2)}) collective-permute-start(f32[2,6,8,128]{3,2,1,0:T(8,128)S(1)} %get-tuple-element.58), channel_id=1, source_target_pairs={{0,1},{1,0},{2,3},{3,2},{4,5},{5,4},{6,7},{7,6},{8,9},{9,8},{10,11... | collective-permute-start | bytes 147464 | tf_op jit(solution)/shard_map/ppermute | solution.py:509
  48.2 0.7 collective-permute-start.11
  48.9 0.9 convolution_bitcast_fusion.refs_7_.refs_14_
  49.8 0.4 shard_map.78.refs_6_.refs_10_
  50.2 0.0 collective-permute-done.10.refs_4_
  50.2 0.0 collective-permute-done.11.refs_5_
  50.2 1.1 shard_map.79
  51.3 4.7 %collective-permute-start.12 = (f32[2,6,8,128]{3,2,1,0:T(8,128)S(1)}, f32[2,6,8,128]{3,2,1,0:T(8,128)S(1)}, u32[]{:S(2)}, u32[]{:S(2)}) collective-permute-start(f32[2,6,8,128]{3,2,1,0:T(8,128)S(1)} %get-tuple-element.62), channel_id=1, source_target_pairs={{0,1},{1,0},{2,3},{3,2},{4,5},{5,4},{6,7},{7,6},{8,9},{9,8},{10,11... | collective-permute-start | bytes 147464 | tf_op jit(solution)/shard_map/ppermute | solution.py:509
  56.0 0.7 collective-permute-start.13
  56.7 0.4 shard_map.80.refs_6_.refs_11_
  57.1 0.4 collective-permute-done.12.refs_4_
  57.5 0.8 shard_map.81.refs_6_.refs_7_
  58.3 0.5 shard_map.82
  58.8 0.1 broadcast_in_dim.6
  58.9 28.7 %all_to_all.10 = f32[32,1,768]{2,1,0:T(1,128)S(1)} all-to-all(f32[32,1,768]{2,1,0:T(1,128)S(1)} %broadcast_in_dim.6), channel_id=1, replica_groups=mesh['slab_0'=4,'slab_1'=16,'slab_2'=2,'sub'=4] {'slab_0','slab_2','sub'}, dimensions={0} | all-to-all | bytes 196608 | tf_op jit(solution)/shard_map/all_to_all | solution.py:22
  87.6 0.1 reduce_sum.9
  87.7 19.4 %all_to_all.11 = f32[16,1,768]{2,1,0:T(1,128)S(1)} all-to-all(f32[16,1,768]{2,1,0:T(1,128)S(1)} %broadcast_in_dim.7), channel_id=1, replica_groups=mesh['slab_0'=4,'slab_1'=16,'slab_2'=2,'sub'=4] {'slab_1'}, dimensions={0} | all-to-all | bytes 98304 | tf_op jit(solution)/shard_map/all_to_all | solution.py:22
  107.1 2.9 %shard_map.83 = (f32[6,6,3,8,128]{4,3,2,1,0:T(8,128)}, f32[6,30]{1,0:T(8,128)}, f32[6,6]{1,0:T(8,128)}) custom-call(f32[16,768]{1,0:T(8,128)S(1)} %bitcast.42, f32[30,6,3,8,128]{4,3,2,1,0:T(8,128)S(1)} %shard_map.69.e_ref.refs_0_.refs_1_, f32[6,3,8,128]{3,2,1,0:T(8,128)S(1)} %get-tuple-element.35.s_ref.refs_0_.refs_1_.refs_2_, ...), custom_call_target="tpu_custom_call" | custom-call | flops 10000000 | bytes 3000000 | tf_op jit(solution)/shard_map/pallas_call | solution.py:454
  (16 shorter events, 0.3 us)
Async XLA Ops:
  2.3 22.9 %collective-permute-start.2 = (bf16[378,8,128]{2,1,0:T(8,128)(2,1)S(1)}, bf16[378,8,128]{2,1,0:T(8,128)(2,1)S(1)}, u32[]{:S(2)}, u32[]{:S(2)}) collective-permute-start(bf16[378,8,128]{2,1,0:T(8,128)(2,1)S(1)} %get-tuple-element.40), channel_id=1, source_target_pairs={{0,4},{4,8},{8,12},{12,16},{16,20},{20,24},{24,28},{28,32},{32,36}... | collective-permute-start | bytes 2322440 | tf_op jit(solution)/shard_map/ppermute | solution.py:487
  7.3 18.0 %collective-permute-start.3 = (bf16[378,8,128]{2,1,0:T(8,128)(2,1)S(1)}, bf16[378,8,128]{2,1,0:T(8,128)(2,1)S(1)}, u32[]{:S(2)}, u32[]{:S(2)}) collective-permute-start(bf16[378,8,128]{2,1,0:T(8,128)(2,1)S(1)} %get-tuple-element.41), channel_id=1, source_target_pairs={{4,0},{8,4},{12,8},{16,12},{20,16},{24,20},{28,24},{32,28},{36,32}... | collective-permute-start | bytes 2322440 | tf_op jit(solution)/shard_map/ppermute | solution.py:488
  12.5 4.8 %collective-permute-start = (f32[6,8,128]{2,1,0:T(8,128)S(1)}, f32[6,8,128]{2,1,0:T(8,128)S(1)}, u32[]{:S(2)}, u32[]{:S(2)}) collective-permute-start(f32[6,8,128]{2,1,0:T(8,128)S(1)} %get-tuple-element.36), channel_id=1, source_target_pairs={{0,1},{1,0},{2,3},{3,2},{4,5},{5,4},{6,7},{7,6},{8,9},{9,8},{10,11... | collective-permute-start | bytes 73736 | tf_op jit(solution)/shard_map/ppermute | solution.py:490
  14.4 2.9 %collective-permute-start.1 = (f32[6,8,128]{2,1,0:T(8,128)S(1)}, f32[6,8,128]{2,1,0:T(8,128)S(1)}, u32[]{:S(2)}, u32[]{:S(2)}) collective-permute-start(f32[6,8,128]{2,1,0:T(8,128)S(1)} %get-tuple-element.37), channel_id=1, source_target_pairs={{1,2},{2,1},{5,6},{6,5},{9,10},{10,9},{13,14},{14,13},{17,18},{18,... | collective-permute-start | bytes 73736 | tf_op jit(solution)/shard_map/ppermute | solution.py:491
  17.3 6.4 %collective-permute-start.4 = (f32[6,4,8,128]{3,2,1,0:T(8,128)S(1)}, f32[6,4,8,128]{3,2,1,0:T(8,128)S(1)}, u32[]{:S(2)}, u32[]{:S(2)}) collective-permute-start(f32[6,4,8,128]{3,2,1,0:T(8,128)S(1)} %get-tuple-element.42), channel_id=1, source_target_pairs={{0,4},{4,8},{8,12},{12,16},{16,20},{20,24},{24,28},{28,32},{32,36}... | collective-permute-start | bytes 294920 | tf_op jit(solution)/shard_map/ppermute | solution.py:496
  19.2 5.9 %collective-permute-start.5 = (f32[6,4,8,128]{3,2,1,0:T(8,128)S(1)}, f32[6,4,8,128]{3,2,1,0:T(8,128)S(1)}, u32[]{:S(2)}, u32[]{:S(2)}) collective-permute-start(f32[6,4,8,128]{3,2,1,0:T(8,128)S(1)} %get-tuple-element.38.after_ref), channel_id=1, source_target_pairs={{4,0},{8,4},{12,8},{16,12},{20,16},{24,20},{28,24},{32,28},{36,32}... | collective-permute-start | bytes 294920 | tf_op jit(solution)/shard_map/ppermute | solution.py:497
  25.2 0.7 copy-start
  27.0 7.5 %collective-permute-start.6 = (f32[2,6,8,128]{3,2,1,0:T(8,128)S(1)}, f32[2,6,8,128]{3,2,1,0:T(8,128)S(1)}, u32[]{:S(2)}, u32[]{:S(2)}) collective-permute-start(f32[2,6,8,128]{3,2,1,0:T(8,128)S(1)} %get-tuple-element.48), channel_id=1, source_target_pairs={{0,1},{1,0},{2,3},{3,2},{4,5},{5,4},{6,7},{7,6},{8,9},{9,8},{10,11... | collective-permute-start | bytes 147464 | tf_op jit(solution)/shard_map/ppermute | solution.py:509
  32.5 2.0 %collective-permute-start.7 = (f32[2,6,8,128]{3,2,1,0:T(8,128)S(1)}, f32[2,6,8,128]{3,2,1,0:T(8,128)S(1)}, u32[]{:S(2)}, u32[]{:S(2)}) collective-permute-start(f32[2,6,8,128]{3,2,1,0:T(8,128)S(1)} %get-tuple-element.49), channel_id=1, source_target_pairs={{1,2},{2,1},{5,6},{6,5},{9,10},{10,9},{13,14},{14,13},{17,18},{18,... | collective-permute-start | bytes 147464 | tf_op jit(solution)/shard_map/ppermute | solution.py:510
  35.6 6.7 %collective-permute-start.8 = (f32[2,6,8,128]{3,2,1,0:T(8,128)S(1)}, f32[2,6,8,128]{3,2,1,0:T(8,128)S(1)}, u32[]{:S(2)}, u32[]{:S(2)}) collective-permute-start(f32[2,6,8,128]{3,2,1,0:T(8,128)S(1)} %get-tuple-element.53), channel_id=1, source_target_pairs={{0,1},{1,0},{2,3},{3,2},{4,5},{5,4},{6,7},{7,6},{8,9},{9,8},{10,11... | collective-permute-start | bytes 147464 | tf_op jit(solution)/shard_map/ppermute | solution.py:509
  40.3 2.0 %collective-permute-start.9 = (f32[2,6,8,128]{3,2,1,0:T(8,128)S(1)}, f32[2,6,8,128]{3,2,1,0:T(8,128)S(1)}, u32[]{:S(2)}, u32[]{:S(2)}) collective-permute-start(f32[2,6,8,128]{3,2,1,0:T(8,128)S(1)} %get-tuple-element.54), channel_id=1, source_target_pairs={{1,2},{2,1},{5,6},{6,5},{9,10},{10,9},{13,14},{14,13},{17,18},{18,... | collective-permute-start | bytes 147464 | tf_op jit(solution)/shard_map/ppermute | solution.py:510
  43.4 6.8 %collective-permute-start.10 = (f32[2,6,8,128]{3,2,1,0:T(8,128)S(1)}, f32[2,6,8,128]{3,2,1,0:T(8,128)S(1)}, u32[]{:S(2)}, u32[]{:S(2)}) collective-permute-start(f32[2,6,8,128]{3,2,1,0:T(8,128)S(1)} %get-tuple-element.58), channel_id=1, source_target_pairs={{0,1},{1,0},{2,3},{3,2},{4,5},{5,4},{6,7},{7,6},{8,9},{9,8},{10,11... | collective-permute-start | bytes 147464 | tf_op jit(solution)/shard_map/ppermute | solution.py:509
  48.2 2.0 %collective-permute-start.11 = (f32[2,6,8,128]{3,2,1,0:T(8,128)S(1)}, f32[2,6,8,128]{3,2,1,0:T(8,128)S(1)}, u32[]{:S(2)}, u32[]{:S(2)}) collective-permute-start(f32[2,6,8,128]{3,2,1,0:T(8,128)S(1)} %get-tuple-element.59), channel_id=1, source_target_pairs={{1,2},{2,1},{5,6},{6,5},{9,10},{10,9},{13,14},{14,13},{17,18},{18,... | collective-permute-start | bytes 147464 | tf_op jit(solution)/shard_map/ppermute | solution.py:510
  51.3 6.2 %collective-permute-start.12 = (f32[2,6,8,128]{3,2,1,0:T(8,128)S(1)}, f32[2,6,8,128]{3,2,1,0:T(8,128)S(1)}, u32[]{:S(2)}, u32[]{:S(2)}) collective-permute-start(f32[2,6,8,128]{3,2,1,0:T(8,128)S(1)} %get-tuple-element.62), channel_id=1, source_target_pairs={{0,1},{1,0},{2,3},{3,2},{4,5},{5,4},{6,7},{7,6},{8,9},{9,8},{10,11... | collective-permute-start | bytes 147464 | tf_op jit(solution)/shard_map/ppermute | solution.py:509
  56.0 1.5 %collective-permute-start.13 = (f32[2,6,8,128]{3,2,1,0:T(8,128)S(1)}, f32[2,6,8,128]{3,2,1,0:T(8,128)S(1)}, u32[]{:S(2)}, u32[]{:S(2)}) collective-permute-start(f32[2,6,8,128]{3,2,1,0:T(8,128)S(1)} %get-tuple-element.63), channel_id=1, source_target_pairs={{1,2},{2,1},{5,6},{6,5},{9,10},{10,9},{13,14},{14,13},{17,18},{18,... | collective-permute-start | bytes 147464 | tf_op jit(solution)/shard_map/ppermute | solution.py:510

commit v3 on v2

--- a/solution.py
+++ b/solution.py
@@ -12,11 +12,6 @@
 EXACT = lax.Precision.HIGHEST
 
 
-def chain(count):
-    up = [(i, i + 1) for i in range(count - 1)]
-    return up, [(b, a) for a, b in up]
-
-
 def all_copies(x, axis):
     copies = jnp.broadcast_to(x, (lax.axis_size(axis), *x.shape))
     return lax.all_to_all(copies, axis, split_axis=0, concat_axis=0, tiled=True)
@@ -34,7 +29,15 @@
     return lax.broadcasted_iota(jnp.int32, shape, len(shape) - 2) < shape[-2] // 2
 
 
-def pack(c_ref, s_ref, own_ref, lo_ref, hi_ref, start_ref, one_ref, two_ref, raw, sems):
+def is_odd():
+    return lax.rem(lax.axis_index("sub"), 2) > 0
+
+
+def is_upper():
+    return lax.axis_index("slab_2") > 0
+
+
+def pack(c_ref, s_ref, own_ref, inner_ref, outer_ref, start_ref, one_ref, two_ref, raw, sems):
     parts = sems.shape[0] - 1
     begin = pltpu.make_async_copy(s_ref, start_ref, sems.at[parts])
     begin.start()
@@ -48,13 +51,16 @@
     for copy in copies:
         copy.start()
     first = half_mask(c_ref.shape[2:])
+    upper = is_upper()
 
     def pair(p, carry):
         a, b = raw[p, 0].astype(jnp.float32), raw[p, 1].astype(jnp.float32)
         own_ref[p, 0] = a
         own_ref[p, 1] = b
-        hi_ref[p] = jnp.where(first, a, swap_halves(b)).astype(hi_ref.dtype)
-        lo_ref[p] = jnp.where(first, swap_halves(a), b).astype(lo_ref.dtype)
+        down = jnp.where(first, a, swap_halves(b))
+        up = jnp.where(first, swap_halves(a), b)
+        inner_ref[p] = jnp.where(upper, down, up).astype(inner_ref.dtype)
+        outer_ref[p] = jnp.where(upper, up, down).astype(outer_ref.dtype)
         return carry
 
     for n, copy in enumerate(copies):
@@ -67,16 +73,18 @@
     two_ref[...] = jnp.where(odd, far, near)
 
 
-def unpack(lo_ref, hi_ref, wide_ref):
-    first = half_mask(lo_ref.shape[1:])
+def unpack(inner_ref, outer_ref, wide_ref):
+    first = half_mask(inner_ref.shape[1:])
+    upper = is_upper()
 
     def pair(p, carry):
-        lo, hi = lo_ref[p].astype(jnp.float32), hi_ref[p].astype(jnp.float32)
+        inner, outer = inner_ref[p].astype(jnp.float32), outer_ref[p].astype(jnp.float32)
+        lo, hi = jnp.where(upper, inner, outer), jnp.where(upper, outer, inner)
         wide_ref[p, 0] = jnp.where(first, hi, swap_halves(lo))
         wide_ref[p, 1] = jnp.where(first, swap_halves(hi), lo)
         return carry
 
-    lax.fori_loop(0, lo_ref.shape[0], pair, 0, unroll=9)
+    lax.fori_loop(0, inner_ref.shape[0], pair, 0, unroll=9)
 
 
 def in_vmem(x):
@@ -119,43 +127,48 @@
     )(in_hbm(pairs), in_hbm(start))
 
 
-def unpacked(lo, hi):
+def unpacked(inner, outer):
     return pl.pallas_call(
         unpack,
-        out_shape=pltpu.VMEM((lo.shape[0], 2, *lo.shape[1:]), jnp.float32),
+        out_shape=pltpu.VMEM((inner.shape[0], 2, *inner.shape[1:]), jnp.float32),
         in_specs=[VMEM] * 2,
         out_specs=VMEM,
         compiler_params=LIMIT,
         cost_estimate=cost(10**6, 4 * 10**6),
-    )(in_vmem(lo), in_vmem(hi))
-
-
-def is_odd():
-    return lax.rem(lax.axis_index("sub"), 2) > 0
-
-
-def both_kernel(s_ref, one_ref, two_ref, up_ref, down_ref):
-    odd = is_odd()
+    )(in_vmem(inner), in_vmem(outer))
+
+
+def both_kernel(s_ref, one_ref, two_ref, after_ref, inner_ref, outer_ref):
+    odd, upper = is_odd(), is_upper()
     columns = s_ref.shape[1]
     low = half_mask(s_ref.shape[2:])
     for e in range(s_ref.shape[0]):
         one, two = one_ref[e], two_ref[e]
         left, right = jnp.where(odd, one, two), jnp.where(odd, two, one)
-        up_ref[e, :columns] = s_ref[e]
-        down_ref[e, :columns] = s_ref[e]
-        up_ref[e, columns] = jnp.where(low, swap_halves(left), right)
-        down_ref[e, columns] = jnp.where(low, left, swap_halves(right))
-
-
-def begin_kernel(s_ref, lo_ref, hi_ref, one_ref, two_ref, v_ref, first_ref, second_ref):
-    odd = is_odd()
+        inner_ref[e, :columns] = s_ref[e]
+        outer_ref[e, :columns] = s_ref[e]
+        up = jnp.where(low, swap_halves(left), right)
+        down = jnp.where(low, left, swap_halves(right))
+        inner_ref[e, columns] = jnp.where(upper, down, up)
+        outer_ref[e, columns] = jnp.where(upper, up, down)
+
+
+def begin_kernel(
+    s_ref, inner_ref, outer_ref, one_ref, two_ref, after_ref, v_ref, first_ref, second_ref
+):
+    odd, upper = is_odd(), is_upper()
     columns = s_ref.shape[1]
     low = half_mask(s_ref.shape[2:])
     for e in range(s_ref.shape[0]):
         for x in range(columns):
             v_ref[0, e, x] = s_ref[e, x]
-            v_ref[1, e, x] = jnp.where(low, hi_ref[e, x], lo_ref[e, x])
-        lo, hi = lo_ref[e, columns], hi_ref[e, columns]
+            v_ref[1, e, x] = jnp.where(
+                upper,
+                jnp.where(low, outer_ref[e, x], inner_ref[e, x]),
+                jnp.where(low, inner_ref[e, x], outer_ref[e, x]),
+            )
+        inner, outer = inner_ref[e, columns], outer_ref[e, columns]
+        lo, hi = jnp.where(upper, inner, outer), jnp.where(upper, outer, inner)
         left = jnp.where(low, hi, swap_halves(lo))
         right = jnp.where(low, swap_halves(hi), lo)
         first_ref[0, e], second_ref[0, e] = one_ref[e], two_ref[e]
@@ -163,15 +176,15 @@
         second_ref[1, e] = jnp.where(odd, right, left)
 
 
-def small_call(kernel, outs, *operands):
+def small_call(kernel, outs, *operands, after=()):
     return pl.pallas_call(
         kernel,
         out_shape=tuple(pltpu.VMEM(shape, jnp.float32) for shape in outs),
-        in_specs=[VMEM] * len(operands),
+        in_specs=[VMEM] * len(operands) + [ANY] * len(after),
         out_specs=(VMEM,) * len(outs),
         compiler_params=LIMIT,
         cost_estimate=cost(10**5, 10**5),
-    )(*(in_vmem(x) for x in operands))
+    )(*(in_vmem(x) for x in operands), *after)
 
 
 def early_kernel(e_ref, after_ref, held_ref, sem):
@@ -195,7 +208,7 @@
 def step_kernel(step, first_step, last_step, shifts_ref, *refs):
     split = len(refs) - (1 if last_step else 3)
     (own_ref, wide_ref, v_ref, one_ref, two_ref, *more), outs = refs[:split], refs[split:]
-    odd = is_odd()
+    odd, upper = is_odd(), is_upper()
     comps, columns = v_ref.shape[1:3]
     rows, lanes = v_ref.shape[3:]
     keep = 1.0 - shifts_ref[step]
@@ -208,7 +221,8 @@
             down, up = pltpu.roll(own, 1, 0), pltpu.roll(own, rows - 1, 0)
             ext_down, ext_up = pltpu.roll(ext, 1, 0), pltpu.roll(ext, rows - 1, 0)
             if first_step:
-                lo, hi = more[0][e, x], more[1][e, x]
+                inner, outer = more[0][e, x], more[1][e, x]
+                lo, hi = jnp.where(upper, inner, outer), jnp.where(upper, outer, inner)
                 low = row < rows // 2
                 wide_down = jnp.where(low, pltpu.roll(hi, 1, 0), pltpu.roll(lo, 1, 0))
                 wide_up = jnp.where(low, pltpu.roll(hi, rows - 1, 0), pltpu.roll(lo, rows - 1, 0))
@@ -479,28 +493,30 @@
     coefficients = jnp.transpose(coefficients, (0, 1, 2, 4, 3, 5))
     earlier = jnp.transpose(earlier, (0, 1, 3, 2, 4))
     start = jnp.transpose(start, (0, 2, 1, 3))
-    up, down = chain(lax.axis_size(SLAB))
+    slabs = lax.axis_size(SLAB)
+    inside = [(i, i ^ 1) for i in range(slabs)]
+    outside = [(i, ((i + 1) ^ 1) - 1) for i in range(1, slabs - 1)]
     columns = lax.axis_size("sub")
     pairs = [(i, i ^ 1) for i in range(columns)]
     between = [(i, ((i + 1) ^ 1) - 1) for i in range(1, columns - 1)]
-    own, lo, hi, start, one, two = packed(coefficients, start)
-    lo = lax.ppermute(lo, SLAB, up)
-    hi = lax.ppermute(hi, SLAB, down)
+    own, inner, outer, start, one, two = packed(coefficients, start)
+    inner = lax.ppermute(inner, SLAB, inside)
+    outer = lax.ppermute(outer, SLAB, outside)
     fields, width, *plane = start.shape
     from_one = lax.ppermute(one, "sub", pairs)
     from_two = lax.ppermute(two, "sub", between)
-    s_lo, s_hi = small_call(
-        both_kernel, [(fields, width + 1, *plane)] * 2, start, from_one, from_two
+    earlier = held(earlier, one)
+    s_inner, s_outer = small_call(
+        both_kernel, [(fields, width + 1, *plane)] * 2, start, from_one, from_two, after=(earlier,)
     )
-    earlier = held(earlier, s_hi)
-    s_lo = lax.ppermute(s_lo, SLAB, up)
-    s_hi = lax.ppermute(s_hi, SLAB, down)
+    s_inner = lax.ppermute(s_inner, SLAB, inside)
+    s_outer = lax.ppermute(s_outer, SLAB, outside)
     own = own.reshape(coefficients.shape)
-    wide = unpacked(lo, hi).reshape(coefficients.shape)
+    wide = unpacked(inner, outer).reshape(coefficients.shape)
     v, from_one, from_two = small_call(
         begin_kernel,
         [(2, *start.shape)] + [(2, fields, *plane)] * 2,
-        start, s_lo, s_hi, from_one, from_two,
+        start, s_inner, s_outer, from_one, from_two, after=(wide,),
     )
     vectors, rows, early = [start], [], []
     thirds = earlier.shape[1] // 3
@@ -508,9 +524,14 @@
         if step:
             from_one = lax.ppermute(one, "sub", pairs)
             from_two = lax.ppermute(two, "sub", between)
-        rows.append(dots(earlier, vectors))
-        more = (s_lo, s_hi) if step == 0 else ()
-        after = [rows[-1]]
+        more = (s_inner, s_outer) if step == 0 else ()
+        after = []
+        if step:
+            rows.append(dots(earlier, vectors))
+            after.append(rows[-1])
+        if step == depth - 1:
+            rows.insert(0, dots(earlier, vectors[:1]))
+            after.append(rows[0])
         if 1 <= step <= 3:
             tied, v = lax.optimization_barrier((earlier, v))
             some = tied[:, (step - 1) * thirds : step * thirds].reshape(tied.shape[0], -1)

time: 111 us -> 107 us (0.964)
  blocking collectives: 48.1 us -> 44.9 us
    all_to_all x2, blocking collectives: 48.1 us -> 44.9 us  [all_copies(): return lax.all_to_all(copies, axis, split_axis=0, concat_axis=0, tiled=True)]
    ppermute x5, starting transfers between devices: 21.6 us -> 18.6 us  [body(): from_one = lax.ppermute(one, 'sub', pairs)]
    ppermute x4, starting transfers between devices: 14.5 us -> 17.4 us  [the longest x1 8.79 us: body(): inner = lax.ppermute(inner, SLAB, inside)]
  transfers between devices with their start and end apart: 14 -> 14, of which waited for: 3 -> 4; matrix products, arithmetic and copies ran while one was open for 3% -> 3% of each run, Pallas kernels for 3% -> 4%
where the time goes in v3:
time: 107 us; the launch traced here: 106 us
  blocking collectives  44.9 us (42%)
  starting transfers between devices  39.3 us (37%)
  Pallas kernels  14.6 us (14%)
  waiting for transfers between devices  3.72 us (3%)
  matrix products  2.6 us (2%)
    all_to_all x2, blocking collectives, all_copies(): return lax.all_to_all(copies, axis, split_axis=0, concat_axis=0, tiled=True)  44.9 us
    ppermute x5, starting transfers between devices, body(): from_one = lax.ppermute(one, 'sub', pairs)  18.6 us
    ppermute x1, starting transfers between devices, body(): inner = lax.ppermute(inner, SLAB, inside)  8.79 us
    pallas_call x5, Pallas kernels, stepped(): pl.pallas_call(lambda *refs: step_kernel(step, step == 0, last, *refs[:6...  5.18 us
    ppermute x1, starting transfers between devices, body(): s_outer = lax.ppermute(s_outer, SLAB, outside)  4.79 us
    ppermute x5, starting transfers between devices, body(): from_two = lax.ppermute(two, 'sub', between)  3.32 us
    pallas_call x1, Pallas kernels, finished(): pl.pallas_call(lambda *refs: finish(block, 1.0 / total, *refs), out_shape...  2.93 us
    dot_general x3, matrix products, body(): jnp.dot(some, some.T, precision=EXACT)  2.6 us
  transfers between devices with their start and end apart: 14, of which 4 were waited for; matrix products, arithmetic and copies ran while one was open for 3% of the time, Pallas kernels for 4%

profile of v3, /device:TPU:1, one launch (start us, length us, event | category | flops | bytes accessed | tf_op | source)
XLA Modules:
  0.0 106.5 jit_solution(6690872212721256045)
XLA Ops:
  0.6 1.8 %shard_map.67 = (f32[378,2,8,128]{3,2,1,0:T(8,128)S(1)}, bf16[378,8,128]{2,1,0:T(8,128)(2,1)S(1)}, bf16[378,8,128]{2,1,0:T(8,128)(2,1)S(1)}, f32[6,3,8,128]{3,2,...) custom-call(bf16[378,2,8,128]{3,2,1,0:T(8,128)(2,1)} %bitcast.45, f32[6,3,8,128]{3,2,1,0:T(8,128)} %bitcast.46), custom_call_target="tpu_custom_call" | custom-call | flops 1000000 | bytes 4000000 | tf_op jit(solution)/shard_map/pallas_call | solution.py:112
  2.4 8.8 %collective-permute-start = (bf16[378,8,128]{2,1,0:T(8,128)(2,1)S(1)}, bf16[378,8,128]{2,1,0:T(8,128)(2,1)S(1)}, u32[]{:S(2)}, u32[]{:S(2)}) collective-permute-start(bf16[378,8,128]{2,1,0:T(8,128)(2,1)S(1)} %get-tuple-element.38), channel_id=1, source_target_pairs={{0,4},{4,0},{8,12},{12,8},{16,20},{20,16},{24,28},{28,24},{32,36},... | collective-permute-start | bytes 2322440 | tf_op jit(solution)/shard_map/ppermute | solution.py:503
  11.2 1.9 %collective-permute-start.1 = (bf16[378,8,128]{2,1,0:T(8,128)(2,1)S(1)}, bf16[378,8,128]{2,1,0:T(8,128)(2,1)S(1)}, u32[]{:S(2)}, u32[]{:S(2)}) collective-permute-start(bf16[378,8,128]{2,1,0:T(8,128)(2,1)S(1)} %get-tuple-element.39), channel_id=1, source_target_pairs={{4,8},{8,4},{12,16},{16,12},{20,24},{24,20},{28,32},{32,28},{36,40... | collective-permute-start | bytes 2322440 | tf_op jit(solution)/shard_map/ppermute | solution.py:504
  13.1 0.7 collective-permute-start.3
  13.8 1.9 %collective-permute-start.2 = (f32[6,8,128]{2,1,0:T(8,128)S(1)}, f32[6,8,128]{2,1,0:T(8,128)S(1)}, u32[]{:S(2)}, u32[]{:S(2)}) collective-permute-start(f32[6,8,128]{2,1,0:T(8,128)S(1)} %get-tuple-element.35.after_ref), channel_id=1, source_target_pairs={{0,1},{1,0},{2,3},{3,2},{4,5},{5,4},{6,7},{7,6},{8,9},{9,8},{10,11... | collective-permute-start | bytes 73736 | tf_op jit(solution)/shard_map/ppermute | solution.py:506
  15.7 1.6 %shard_map.68.after_ref.e_ref.refs_0_.refs_1_ = f32[30,6,3,8,128]{4,3,2,1,0:T(8,128)S(1)} custom-call(f32[30,6,3,8,128]{4,3,2,1,0:T(8,128)} %bitcast.44, f32[6,8,128]{2,1,0:T(8,128)S(1)} %get-tuple-element.35.after_ref), custom_call_target="tpu_custom_call" | custom-call | flops 100000 | bytes 5000000 | tf_op jit(solution)/shard_map/pallas_call | solution.py:197
  17.4 0.0 collective-permute-done.3.two_ref
  17.4 1.0 collective-permute-done.2.one_ref
  18.4 1.9 %collective-permute-start.4 = (f32[6,4,8,128]{3,2,1,0:T(8,128)S(1)}, f32[6,4,8,128]{3,2,1,0:T(8,128)S(1)}, u32[]{:S(2)}, u32[]{:S(2)}) collective-permute-start(f32[6,4,8,128]{3,2,1,0:T(8,128)S(1)} %get-tuple-element.41), channel_id=1, source_target_pairs={{0,4},{4,0},{8,12},{12,8},{16,20},{20,16},{24,28},{28,24},{32,36},... | collective-permute-start | bytes 294920 | tf_op jit(solution)/shard_map/ppermute | solution.py:512
  20.3 4.8 %collective-permute-start.5 = (f32[6,4,8,128]{3,2,1,0:T(8,128)S(1)}, f32[6,4,8,128]{3,2,1,0:T(8,128)S(1)}, u32[]{:S(2)}, u32[]{:S(2)}) collective-permute-start(f32[6,4,8,128]{3,2,1,0:T(8,128)S(1)} %get-tuple-element.42), channel_id=1, source_target_pairs={{4,8},{8,4},{12,16},{16,12},{20,24},{24,20},{28,32},{32,28},{36,40... | collective-permute-start | bytes 294920 | tf_op jit(solution)/shard_map/ppermute | solution.py:513
  25.1 0.4 shard_map.80.refs_7_
  25.5 0.0 collective-permute-done.inner_ref
  25.5 0.0 collective-permute-done.1.outer_ref
  25.5 0.6 shard_map.69
  26.1 0.0 copy-start
  26.1 1.3 %collective-permute-done.5.outer_ref.refs_7_ = f32[6,4,8,128]{3,2,1,0:T(8,128)S(1)} collective-permute-done((f32[6,4,8,128]{3,2,1,0:T(8,128)S(1)}, f32[6,4,8,128]{3,2,1,0:T(8,128)S(1)}, u32[]{:S(2)}, u32[]{:S(2)}) %collective-permute-start.5) | collective-permute-done | bytes 98336 | tf_op jit(solution)/shard_map/ppermute | solution.py:513
  27.4 1.1 %shard_map.72 = (f32[2,6,3,8,128]{4,3,2,1,0:T(8,128)S(1)}, f32[2,6,8,128]{3,2,1,0:T(8,128)S(1)}, f32[2,6,8,128]{3,2,1,0:T(8,128)S(1)}) custom-call(f32[5]{0:T(128)S(1)} %copy-done, f32[7,6,6,3,8,128]{5,4,3,2,1,0:T(8,128)S(1)} %bitcast.38, f32[7,6,6,3,8,128]{5,4,3,2,1,0:T(8,128)S(1)} %bitcast.33, f32[2,6,3,8,128]{4,3,2,1,0:T(8,128)S(1)} %get-tuple-element.43.refs_3_, ...), custom_call_target="tpu_custom_call" | custom-call | flops 10000000 | bytes 3000000 | tf_op jit(solution)/shard_map/pallas_call | solution.py:274
  28.6 1.9 %collective-permute-start.6 = (f32[2,6,8,128]{3,2,1,0:T(8,128)S(1)}, f32[2,6,8,128]{3,2,1,0:T(8,128)S(1)}, u32[]{:S(2)}, u32[]{:S(2)}) collective-permute-start(f32[2,6,8,128]{3,2,1,0:T(8,128)S(1)} %get-tuple-element.48), channel_id=1, source_target_pairs={{0,1},{1,0},{2,3},{3,2},{4,5},{5,4},{6,7},{7,6},{8,9},{9,8},{10,11... | collective-permute-start | bytes 147464 | tf_op jit(solution)/shard_map/ppermute | solution.py:525
  30.5 0.7 collective-permute-start.7
  31.2 0.9 convolution_bitcast_fusion.2.refs_7_.refs_12_
  32.1 0.4 shard_map.73.refs_6_.refs_8_
  32.5 0.9 collective-permute-done.6.refs_4_
  33.4 1.1 shard_map.74
  34.5 5.3 %collective-permute-start.8 = (f32[2,6,8,128]{3,2,1,0:T(8,128)S(1)}, f32[2,6,8,128]{3,2,1,0:T(8,128)S(1)}, u32[]{:S(2)}, u32[]{:S(2)}) collective-permute-start(f32[2,6,8,128]{3,2,1,0:T(8,128)S(1)} %get-tuple-element.53), channel_id=1, source_target_pairs={{0,1},{1,0},{2,3},{3,2},{4,5},{5,4},{6,7},{7,6},{8,9},{9,8},{10,11... | collective-permute-start | bytes 147464 | tf_op jit(solution)/shard_map/ppermute | solution.py:525
  39.8 0.7 collective-permute-start.9
  40.5 0.9 convolution_bitcast_fusion.1.refs_7_.refs_13_
  41.4 0.4 shard_map.75.refs_6_.refs_9_
  41.8 0.0 collective-permute-done.8.refs_4_
  41.8 0.0 collective-permute-done.9.refs_5_
  41.8 1.1 %shard_map.76 = (f32[2,6,3,8,128]{4,3,2,1,0:T(8,128)S(1)}, f32[2,6,8,128]{3,2,1,0:T(8,128)S(1)}, f32[2,6,8,128]{3,2,1,0:T(8,128)S(1)}) custom-call(f32[5]{0:T(128)S(1)} %copy-done, f32[7,6,6,3,8,128]{5,4,3,2,1,0:T(8,128)S(1)} %bitcast.40, f32[7,6,6,3,8,128]{5,4,3,2,1,0:T(8,128)S(1)} %bitcast.35, f32[2,6,3,8,128]{4,3,2,1,0:T(8,128)S(1)} %get-tuple-element.52.refs_3_, ...), custom_call_target="tpu_custom_call" | custom-call | flops 10000000 | bytes 3000000 | tf_op jit(solution)/shard_map/pallas_call | solution.py:274
  42.9 4.7 %collective-permute-start.10 = (f32[2,6,8,128]{3,2,1,0:T(8,128)S(1)}, f32[2,6,8,128]{3,2,1,0:T(8,128)S(1)}, u32[]{:S(2)}, u32[]{:S(2)}) collective-permute-start(f32[2,6,8,128]{3,2,1,0:T(8,128)S(1)} %get-tuple-element.58), channel_id=1, source_target_pairs={{0,1},{1,0},{2,3},{3,2},{4,5},{5,4},{6,7},{7,6},{8,9},{9,8},{10,11... | collective-permute-start | bytes 147464 | tf_op jit(solution)/shard_map/ppermute | solution.py:525
  47.6 0.7 collective-permute-start.11
  48.4 0.9 convolution_bitcast_fusion.refs_7_.refs_14_
  49.2 0.4 shard_map.77.refs_6_.refs_10_
  49.6 0.0 collective-permute-done.10.refs_4_
  49.6 0.0 collective-permute-done.11.refs_5_
  49.6 1.1 %shard_map.78 = (f32[2,6,3,8,128]{4,3,2,1,0:T(8,128)S(1)}, f32[2,6,8,128]{3,2,1,0:T(8,128)S(1)}, f32[2,6,8,128]{3,2,1,0:T(8,128)S(1)}) custom-call(f32[5]{0:T(128)S(1)} %copy-done, f32[7,6,6,3,8,128]{5,4,3,2,1,0:T(8,128)S(1)} %bitcast.41, f32[7,6,6,3,8,128]{5,4,3,2,1,0:T(8,128)S(1)} %bitcast.36, f32[2,6,3,8,128]{4,3,2,1,0:T(8,128)S(1)} %get-tuple-element.57.refs_3_, ...), custom_call_target="tpu_custom_call" | custom-call | flops 10000000 | bytes 3000000 | tf_op jit(solution)/shard_map/pallas_call | solution.py:274
  50.7 4.7 %collective-permute-start.12 = (f32[2,6,8,128]{3,2,1,0:T(8,128)S(1)}, f32[2,6,8,128]{3,2,1,0:T(8,128)S(1)}, u32[]{:S(2)}, u32[]{:S(2)}) collective-permute-start(f32[2,6,8,128]{3,2,1,0:T(8,128)S(1)} %get-tuple-element.62), channel_id=1, source_target_pairs={{0,1},{1,0},{2,3},{3,2},{4,5},{5,4},{6,7},{7,6},{8,9},{9,8},{10,11... | collective-permute-start | bytes 147464 | tf_op jit(solution)/shard_map/ppermute | solution.py:525
  55.5 0.7 collective-permute-start.13
  56.1 0.4 shard_map.79.refs_6_.refs_11_
  56.5 0.5 collective-permute-done.12.refs_4_
  57.1 0.8 shard_map.81.refs_6_.refs_7_
  57.9 0.5 shard_map.82
  58.4 0.1 broadcast_in_dim.6
  58.5 28.7 %all_to_all.10 = f32[32,1,768]{2,1,0:T(1,128)S(1)} all-to-all(f32[32,1,768]{2,1,0:T(1,128)S(1)} %broadcast_in_dim.6), channel_id=1, replica_groups=mesh['slab_0'=4,'slab_1'=16,'slab_2'=2,'sub'=4] {'slab_0','slab_2','sub'}, dimensions={0} | all-to-all | bytes 196608 | tf_op jit(solution)/shard_map/all_to_all | solution.py:17
  87.2 0.1 reduce_sum.9
  87.3 16.3 %all_to_all.11 = f32[16,1,768]{2,1,0:T(1,128)S(1)} all-to-all(f32[16,1,768]{2,1,0:T(1,128)S(1)} %broadcast_in_dim.7), channel_id=1, replica_groups=mesh['slab_0'=4,'slab_1'=16,'slab_2'=2,'sub'=4] {'slab_1'}, dimensions={0} | all-to-all | bytes 98304 | tf_op jit(solution)/shard_map/all_to_all | solution.py:17
  103.5 2.9 %shard_map.83 = (f32[6,6,3,8,128]{4,3,2,1,0:T(8,128)}, f32[6,30]{1,0:T(8,128)}, f32[6,6]{1,0:T(8,128)}) custom-call(f32[16,768]{1,0:T(8,128)S(1)} %bitcast.43, f32[30,6,3,8,128]{4,3,2,1,0:T(8,128)S(1)} %shard_map.68.after_ref.e_ref.refs_0_.refs_1_, f32[6,3,8,128]{3,2,1,0:T(8,128)S(1)} %get-tuple-element.36.s_ref.refs_0_.refs_1_.refs_2_, ...), custom_call_target="tpu_custom_call" | custom-call | flops 10000000 | bytes 3000000 | tf_op jit(solution)/shard_map/pallas_call | solution.py:468
  (16 shorter events, 0.3 us)
Async XLA Ops:
  2.4 23.1 %collective-permute-start = (bf16[378,8,128]{2,1,0:T(8,128)(2,1)S(1)}, bf16[378,8,128]{2,1,0:T(8,128)(2,1)S(1)}, u32[]{:S(2)}, u32[]{:S(2)}) collective-permute-start(bf16[378,8,128]{2,1,0:T(8,128)(2,1)S(1)} %get-tuple-element.38), channel_id=1, source_target_pairs={{0,4},{4,0},{8,12},{12,8},{16,20},{20,16},{24,28},{28,24},{32,36},... | collective-permute-start | bytes 2322440 | tf_op jit(solution)/shard_map/ppermute | solution.py:503
  11.2 14.3 %collective-permute-start.1 = (bf16[378,8,128]{2,1,0:T(8,128)(2,1)S(1)}, bf16[378,8,128]{2,1,0:T(8,128)(2,1)S(1)}, u32[]{:S(2)}, u32[]{:S(2)}) collective-permute-start(bf16[378,8,128]{2,1,0:T(8,128)(2,1)S(1)} %get-tuple-element.39), channel_id=1, source_target_pairs={{4,8},{8,4},{12,16},{16,12},{20,24},{24,20},{28,32},{32,28},{36,40... | collective-permute-start | bytes 2322440 | tf_op jit(solution)/shard_map/ppermute | solution.py:504
  13.1 4.2 %collective-permute-start.3 = (f32[6,8,128]{2,1,0:T(8,128)S(1)}, f32[6,8,128]{2,1,0:T(8,128)S(1)}, u32[]{:S(2)}, u32[]{:S(2)}) collective-permute-start(f32[6,8,128]{2,1,0:T(8,128)S(1)} %get-tuple-element.40), channel_id=1, source_target_pairs={{1,2},{2,1},{5,6},{6,5},{9,10},{10,9},{13,14},{14,13},{17,18},{18,... | collective-permute-start | bytes 73736 | tf_op jit(solution)/shard_map/ppermute | solution.py:507
  13.8 4.6 %collective-permute-start.2 = (f32[6,8,128]{2,1,0:T(8,128)S(1)}, f32[6,8,128]{2,1,0:T(8,128)S(1)}, u32[]{:S(2)}, u32[]{:S(2)}) collective-permute-start(f32[6,8,128]{2,1,0:T(8,128)S(1)} %get-tuple-element.35.after_ref), channel_id=1, source_target_pairs={{0,1},{1,0},{2,3},{3,2},{4,5},{5,4},{6,7},{7,6},{8,9},{9,8},{10,11... | collective-permute-start | bytes 73736 | tf_op jit(solution)/shard_map/ppermute | solution.py:506
  18.4 7.7 %collective-permute-start.4 = (f32[6,4,8,128]{3,2,1,0:T(8,128)S(1)}, f32[6,4,8,128]{3,2,1,0:T(8,128)S(1)}, u32[]{:S(2)}, u32[]{:S(2)}) collective-permute-start(f32[6,4,8,128]{3,2,1,0:T(8,128)S(1)} %get-tuple-element.41), channel_id=1, source_target_pairs={{0,4},{4,0},{8,12},{12,8},{16,20},{20,16},{24,28},{28,24},{32,36},... | collective-permute-start | bytes 294920 | tf_op jit(solution)/shard_map/ppermute | solution.py:512
  20.3 7.1 %collective-permute-start.5 = (f32[6,4,8,128]{3,2,1,0:T(8,128)S(1)}, f32[6,4,8,128]{3,2,1,0:T(8,128)S(1)}, u32[]{:S(2)}, u32[]{:S(2)}) collective-permute-start(f32[6,4,8,128]{3,2,1,0:T(8,128)S(1)} %get-tuple-element.42), channel_id=1, source_target_pairs={{4,8},{8,4},{12,16},{16,12},{20,24},{24,20},{28,32},{32,28},{36,40... | collective-permute-start | bytes 294920 | tf_op jit(solution)/shard_map/ppermute | solution.py:513
  26.1 1.3 %copy-start = (f32[5]{0:T(128)S(1)}, f32[5]{0:T(128)}, u32[]{:S(2)}) copy-start(f32[5]{0:T(128)} %refs_0_.9) | copy-start | bytes 64
  28.6 4.8 %collective-permute-start.6 = (f32[2,6,8,128]{3,2,1,0:T(8,128)S(1)}, f32[2,6,8,128]{3,2,1,0:T(8,128)S(1)}, u32[]{:S(2)}, u32[]{:S(2)}) collective-permute-start(f32[2,6,8,128]{3,2,1,0:T(8,128)S(1)} %get-tuple-element.48), channel_id=1, source_target_pairs={{0,1},{1,0},{2,3},{3,2},{4,5},{5,4},{6,7},{7,6},{8,9},{9,8},{10,11... | collective-permute-start | bytes 147464 | tf_op jit(solution)/shard_map/ppermute | solution.py:525
  30.5 2.9 %collective-permute-start.7 = (f32[2,6,8,128]{3,2,1,0:T(8,128)S(1)}, f32[2,6,8,128]{3,2,1,0:T(8,128)S(1)}, u32[]{:S(2)}, u32[]{:S(2)}) collective-permute-start(f32[2,6,8,128]{3,2,1,0:T(8,128)S(1)} %get-tuple-element.49), channel_id=1, source_target_pairs={{1,2},{2,1},{5,6},{6,5},{9,10},{10,9},{13,14},{14,13},{17,18},{18,... | collective-permute-start | bytes 147464 | tf_op jit(solution)/shard_map/ppermute | solution.py:526
  34.5 7.3 %collective-permute-start.8 = (f32[2,6,8,128]{3,2,1,0:T(8,128)S(1)}, f32[2,6,8,128]{3,2,1,0:T(8,128)S(1)}, u32[]{:S(2)}, u32[]{:S(2)}) collective-permute-start(f32[2,6,8,128]{3,2,1,0:T(8,128)S(1)} %get-tuple-element.53), channel_id=1, source_target_pairs={{0,1},{1,0},{2,3},{3,2},{4,5},{5,4},{6,7},{7,6},{8,9},{9,8},{10,11... | collective-permute-start | bytes 147464 | tf_op jit(solution)/shard_map/ppermute | solution.py:525
  39.8 2.0 %collective-permute-start.9 = (f32[2,6,8,128]{3,2,1,0:T(8,128)S(1)}, f32[2,6,8,128]{3,2,1,0:T(8,128)S(1)}, u32[]{:S(2)}, u32[]{:S(2)}) collective-permute-start(f32[2,6,8,128]{3,2,1,0:T(8,128)S(1)} %get-tuple-element.54), channel_id=1, source_target_pairs={{1,2},{2,1},{5,6},{6,5},{9,10},{10,9},{13,14},{14,13},{17,18},{18,... | collective-permute-start | bytes 147464 | tf_op jit(solution)/shard_map/ppermute | solution.py:526
  42.9 6.7 %collective-permute-start.10 = (f32[2,6,8,128]{3,2,1,0:T(8,128)S(1)}, f32[2,6,8,128]{3,2,1,0:T(8,128)S(1)}, u32[]{:S(2)}, u32[]{:S(2)}) collective-permute-start(f32[2,6,8,128]{3,2,1,0:T(8,128)S(1)} %get-tuple-element.58), channel_id=1, source_target_pairs={{0,1},{1,0},{2,3},{3,2},{4,5},{5,4},{6,7},{7,6},{8,9},{9,8},{10,11... | collective-permute-start | bytes 147464 | tf_op jit(solution)/shard_map/ppermute | solution.py:525
  47.6 2.0 %collective-permute-start.11 = (f32[2,6,8,128]{3,2,1,0:T(8,128)S(1)}, f32[2,6,8,128]{3,2,1,0:T(8,128)S(1)}, u32[]{:S(2)}, u32[]{:S(2)}) collective-permute-start(f32[2,6,8,128]{3,2,1,0:T(8,128)S(1)} %get-tuple-element.59), channel_id=1, source_target_pairs={{1,2},{2,1},{5,6},{6,5},{9,10},{10,9},{13,14},{14,13},{17,18},{18,... | collective-permute-start | bytes 147464 | tf_op jit(solution)/shard_map/ppermute | solution.py:526
  50.7 6.3 %collective-permute-start.12 = (f32[2,6,8,128]{3,2,1,0:T(8,128)S(1)}, f32[2,6,8,128]{3,2,1,0:T(8,128)S(1)}, u32[]{:S(2)}, u32[]{:S(2)}) collective-permute-start(f32[2,6,8,128]{3,2,1,0:T(8,128)S(1)} %get-tuple-element.62), channel_id=1, source_target_pairs={{0,1},{1,0},{2,3},{3,2},{4,5},{5,4},{6,7},{7,6},{8,9},{9,8},{10,11... | collective-permute-start | bytes 147464 | tf_op jit(solution)/shard_map/ppermute | solution.py:525
  55.5 1.6 %collective-permute-start.13 = (f32[2,6,8,128]{3,2,1,0:T(8,128)S(1)}, f32[2,6,8,128]{3,2,1,0:T(8,128)S(1)}, u32[]{:S(2)}, u32[]{:S(2)}) collective-permute-start(f32[2,6,8,128]{3,2,1,0:T(8,128)S(1)} %get-tuple-element.63), channel_id=1, source_target_pairs={{1,2},{2,1},{5,6},{6,5},{9,10},{10,9},{13,14},{14,13},{17,18},{18,... | collective-permute-start | bytes 147464 | tf_op jit(solution)/shard_map/ppermute | solution.py:526
